TPU v7x, 32 devices: a whole 2x2x4 slice. The times are simulated.
32 devices in a mesh: groups: 2 (over x), src: 8 (over z, y), tile: 2 (over core).
Axes of the slice: x: 2, y: 2, z: 4, core: 2. Of those that a mesh axis runs over, the one named last changes fastest.
Arguments:
- mask: float32 [2048, 1024], P(('groups', 'tile')), parts along dimension 0, may hold values from 0 to 1
- target: float32 [2048, 1024], P(('groups', 'tile')), parts along dimension 0, may hold values from 0 to 1
- pupil: float32 [64, 64], replicated, may hold values from 0.1 to 1.9
- source_shift: int32 [24, 2], replicated, may hold values from -24 to 24
- source_weight: float32 [24], replicated, may hold values from 0.25 to 4
Outputs:
- mask_gradient: float32 [2048, 1024], P(('groups', 'tile'), 'src'), parts along dimension 0
There are 2 independent parts, one for each index of `groups`. A program takes and returns all parts, laid end to end along the dimension named above; an argument that names none is the same for every part. Nothing has to cross between parts.
Inputs may be any that keep to these rules, and one draw needn't show every extreme that they name: `source_shift`: integer frequency shifts of the source points.
All inputs are finite; a program needn't handle non-finite values.
Results may differ from a plain program's by a relative error of at most 0.0003.
Values sent between devices are 32-bit elements; how exact they have to be, the bound alone decides.
No kernel may reach another device: no remote copies, remote signals or barrier semaphores. Data moves between devices by JAX's collectives and lax.ppermute only.
A program may use at most 128 MiB of HBM per device.

v0:
```python
import functools
import math

import jax
import jax.numpy as jnp
import ml_dtypes
import numpy as np
from jax import lax
from jax.experimental import pallas as pl
from jax.experimental.pallas import tpu as pltpu
from jax.sharding import PartitionSpec as P

TS = 512
HALO = 64
PAD = TS + 2 * HALO
LANES = 128
SKEW = 12
FINE = 512
MOST = 24

resist_gain = 25.0
resist_level = 0.25

f32 = jnp.float32
bf16 = jnp.bfloat16


def halves(table):
    table = np.asarray(table, np.float64)
    high = table.astype(np.float32).astype(ml_dtypes.bfloat16)
    low = (table - high.astype(np.float64)).astype(np.float32).astype(ml_dtypes.bfloat16)
    return high, low


def turns(left, right, period):
    angle = 2.0 * np.pi * np.mod(np.outer(left, right), period) / period
    return np.cos(angle), np.sin(angle)


def both(table, axis):
    return np.concatenate(halves(table), axis=axis)


def split(value):
    high = value.astype(bf16)
    return high, (value - high.astype(f32)).astype(bf16)


def dot(left, right):
    return lax.dot_general(left, right, (((1,), (0,)), ((), ())), preferred_element_type=f32)


class Plan:
    def __init__(self, freqs, cols, n_src, sources):
        self.freqs = freqs
        self.reach = (3 * freqs) // 8
        self.band = 2 * freqs
        self.coarse = 2 * freqs
        self.cols = cols
        self.tile_cols = cols // TS
        self.width = cols // n_src
        self.wide = -(-self.width // LANES) * LANES
        self.n_src = n_src
        self.sources = sources
        self.group = max(n for n in range(2, MOST + 1, 2) if sources % n == 0)
        self.stores = self.tile_cols if sources <= MOST else 1
        self.spans = [
            (max(0, c * TS - LANES), min(cols, (c + 1) * TS + LANES)) for c in range(self.tile_cols)
        ]

    def tables(self):
        freqs, band, coarse = self.freqs, self.band, self.coarse
        index = np.arange(band)
        used = (index < freqs + 2 * self.reach).astype(np.float64)
        centre = index - (freqs // 2 + self.reach)
        out = {}
        cosine, sine = turns(centre, np.arange(PAD), PAD)
        rows = np.concatenate([cosine, -sine], axis=0) * np.concatenate([used, used])[:, None]
        out["e_own"] = both(rows[:, HALO : HALO + TS], 0)
        out["e_rim"] = np.stack([both(rows[:, HALO + TS :], 0), both(rows[:, :HALO], 0)])
        out["final_rows"] = np.stack(halves(rows.T))

        def fold(real, imag):
            return np.concatenate(
                [real[:, :freqs], imag[:, :freqs], real[:, freqs:], imag[:, freqs:]], axis=1
            )

        for c, (first, last) in enumerate(self.spans):
            place = np.arange(first, last) - c * TS + HALO
            inside = ((place >= 0) & (place < PAD)).astype(np.float64)[:, None] * used
            cosine, sine = turns(place, centre, PAD)
            cosine, sine = cosine * inside, sine * inside
            out[f"col{c}"] = both(np.concatenate([fold(cosine, -sine), fold(sine, cosine)], axis=0), 1)
        relative = np.arange(freqs) - freqs // 2
        points = np.arange(coarse)
        cosine, sine = turns(points, relative, coarse)
        high, low = halves(np.concatenate([cosine, -sine], axis=1))
        out["up_rows"] = np.concatenate(
            [np.concatenate([high, high], axis=1), np.concatenate([low, low], axis=1)], axis=0
        )
        high, low = halves(np.concatenate([cosine.T, sine.T], axis=0))
        out["down_rows"] = np.concatenate(
            [np.concatenate([high, high], axis=1), np.concatenate([low, low], axis=1)], axis=0
        )
        order = np.concatenate([points[::2], points[1::2]])
        up, down = [], []
        for some in (points[::2], points[1::2]):
            cosine, sine = turns(centre[:freqs], some, coarse)
            table = np.concatenate(
                [np.concatenate([cosine, sine], axis=1), np.concatenate([-sine, cosine], axis=1)], axis=0
            )
            for into, piece in ((up, table), (down, table.T)):
                pair = both(piece, 1)
                into.append(np.concatenate([pair, pair], axis=0))
        out["up_cols"], out["down_cols"] = np.stack(up), np.stack(down)
        spread = (np.arange(TS) + HALO)[:, None] - (PAD // coarse) * points[None, :]
        weave = np.ones(spread.shape)
        for p in range(1, freqs):
            weave = weave + 2.0 * np.cos(2.0 * np.pi * np.mod(p * spread, PAD) / PAD)
        weave = weave / coarse
        out["weave_rows"] = both(weave, 1)
        out["weave_cols"] = both(weave[:, order], 1)
        turned = both(weave[:, order].T, 1)
        out["weave_up"] = np.concatenate([turned, turned], axis=0)
        out["weave_down"] = both(weave.T, 0)
        blocks = []
        for j in range(self.n_src):
            pieces = []
            for c in range(self.tile_cols):
                place = np.arange(j * self.width, (j + 1) * self.width) - c * TS + HALO
                inside = ((place >= 0) & (place < PAD)).astype(np.float64)[:, None] * used
                cosine = np.zeros((self.wide, band))
                sine = np.zeros((self.wide, band))
                cosine[: self.width], sine[: self.width] = turns(place, centre, PAD)
                cosine[: self.width] *= inside
                sine[: self.width] *= inside
                pieces.append(
                    np.concatenate([fold(cosine, -sine), fold(sine, cosine)], axis=0).T
                )
            blocks.append(both(np.concatenate(pieces, axis=0), 1))
        out["final_cols"] = np.stack(blocks)
        return {name: np.ascontiguousarray(value) for name, value in out.items()}


def skewed(stages, count, gap):
    for step in range(count + gap * (len(stages) - 1)):
        for late, stage in reversed(list(enumerate(stages))):
            if 0 <= step - late * gap < count:
                stage(step - late * gap)


def image_kernel(plan, names, shift, weight, pupil, mask, target, halo, *refs):
    tabs = dict(zip(names, refs[: len(names)]))
    own_out, row_out = refs[len(names) : len(names) + 2]
    (
        mask_v, target_v, e_rim, final_tab, pupils, spectrum, fields, grads, whole_grad,
        u_high, u_low, woven, lifts, lines, sems,
    ) = refs[len(names) + 2 :]
    sources, group = plan.sources, plan.group
    freqs, reach, band, coarse = plan.freqs, plan.reach, plan.band, plan.coarse
    tile_row = lax.axis_index("tile")
    block = lax.axis_index("src")
    copies = [
        pltpu.make_async_copy(mask, mask_v, sems.at[0]),
        pltpu.make_async_copy(tabs["e_rim"].at[tile_row], e_rim, sems.at[1]),
        pltpu.make_async_copy(target, target_v, sems.at[2]),
        pltpu.make_async_copy(tabs["final_cols"].at[block], final_tab, sems.at[3]),
    ]
    for copy in copies:
        copy.start()
    total = weight[0]
    for s in range(1, sources):
        total = total + weight[s]
    share = 1.0 / total
    lane = lax.broadcasted_iota(jnp.int32, (1, band), 1)
    first_half = lane < freqs
    residue = jnp.where(first_half, lane, lane - freqs)
    sign = jnp.where(first_half, 1.0, -1.0).astype(f32)
    doubled = jnp.concatenate([pupil[...], pupil[...]], axis=1)

    def place_pupil(s):
        pupils[s] = pltpu.roll(doubled, shift[1, s] + reach, 1)

    if sources <= MOST:
        for s in range(sources):
            place_pupil(s)
    else:
        lax.fori_loop(0, sources, lambda s, c: (place_pupil(s), c)[1], 0)

    copies[0].wait()
    copies[1].wait()
    e_own, rim_table = tabs["e_own"], e_rim[...]
    for n in range(0, plan.cols, 256):
        high, low = split(mask_v[:, n : n + 256])
        rim_high, rim_low = split(halo[:, n : n + 256])
        part = dot(e_own[...], high) + dot(rim_table, rim_high)
        rows = part[: 2 * band] + part[2 * band :]
        rows = rows + dot(e_own[: 2 * band, :], low) + dot(rim_table[: 2 * band], rim_low)
        high, low = split(rows)
        u_high[:, n : n + 256] = high
        u_low[:, n : n + 256] = low
    scale = 1.0 / (PAD * PAD)
    for c, (first, last) in enumerate(plan.spans):
        high = jnp.concatenate([u_high[:band, first:last], u_high[band:, first:last]], axis=1)
        low = jnp.concatenate([u_low[:band, first:last], u_low[band:, first:last]], axis=1)
        prod = dot(high, tabs[f"col{c}"][...])
        prod = prod[:, : 2 * band] + prod[:, 2 * band :] + dot(low, tabs[f"col{c}"][:, : 2 * band])
        prod = prod * scale
        for k in range(2):
            half = prod[:, k * band : (k + 1) * band]
            spectrum[c, k] = half
            spectrum[c, 2 + k] = pltpu.roll(half, freqs, 1) * sign

    def lane_block(value, k):
        return value[:, k * band : (k + 1) * band]

    pairs = group // 2

    def forward(c, first, power):
        state = {"p": power}
        keep = c % plan.stores

        def gather(i):
            for k in (2 * i, 2 * i + 1):
                down = shift[0, first + k] + reach
                along = shift[1, first + k] + reach
                rows = pl.ds(down, freqs)
                near = residue >= along
                upper = jnp.where(near, spectrum[c, 0, rows, :], spectrum[c, 1, rows, :])
                lower = jnp.where(near, spectrum[c, 2, rows, :], spectrum[c, 3, rows, :])
                scaled = pupils[first + k]
                high, low = split(jnp.concatenate([upper * scaled, lower * scaled], axis=0))
                lifts[:band, k * band : (k + 1) * band] = high
                lifts[band:, k * band : (k + 1) * band] = low

        def lift(i):
            lifted = dot(tabs["up_rows"][...], lifts[:, 2 * i * band : 2 * (i + 1) * band])
            high, low = split(lifted[:coarse] + lifted[coarse:])
            for k in range(2):
                lines[2 * i + k, :, :band] = lane_block(high, k)
                lines[2 * i + k, :, band:] = lane_block(low, k)

        def light_up(i):
            for k in (2 * i, 2 * i + 1):
                along = shift[1, first + k] + reach
                flip = jnp.where(residue >= along, 1.0, -1.0).astype(bf16)
                line = lines[k]
                even = dot(line, tabs["up_cols"][0])
                odd = dot(line * jnp.concatenate([flip, flip], axis=1), tabs["up_cols"][1])
                field = jnp.concatenate(
                    [even[:, :coarse] + even[:, coarse:], odd[:, :coarse] + odd[:, coarse:]], axis=1
                )
                fields[keep, first + k] = field
                state["p"] = state["p"] + weight[first + k] * (field * field)

        skewed([gather, lift, light_up], pairs, SKEW)
        return state["p"]

    def fine(c, power):
        even, odd = power[:, :coarse], power[:, coarse:]
        power = jnp.where(first_half, even + pltpu.roll(even, freqs, 1), odd + pltpu.roll(odd, freqs, 1))
        high, low = split(power * share)
        power_pair = jnp.concatenate([high, low], axis=1)
        power_quad = jnp.concatenate([power_pair, power_pair], axis=0)
        state = {}

        def rows_of(m):
            return slice(m * FINE, (m + 1) * FINE)

        def weave_rows(m):
            left = dot(tabs["weave_rows"][rows_of(m), :], power_quad)
            high, low = split(left[:, :coarse] + left[:, coarse:])
            state["a", m] = jnp.concatenate([high, low], axis=1)

        def slope_rows(m):
            light = dot(state.pop(("a", m)), tabs["weave_up"][...])
            light = light[:, :TS] + light[:, TS:]
            printed = 1.0 / (1.0 + jnp.exp(-resist_gain * (light - resist_level)))
            wanted = target_v[rows_of(m), c * TS : (c + 1) * TS]
            slope = (2.0 * resist_gain) * (printed - wanted) * printed * (1.0 - printed)
            state["g", m] = split(slope)

        def fold_rows(m):
            high, low = state.pop(("g", m))
            part = dot(high, tabs["weave_cols"][...]) + dot(low, tabs["weave_cols"][...])
            high, low = split(part[:, :coarse] + part[:, coarse:])
            woven[rows_of(m), :] = jnp.concatenate([high, low], axis=1)

        skewed([weave_rows, slope_rows, fold_rows], TS // FINE, 1)
        part = dot(tabs["weave_down"][...], woven[...])
        part = part[:coarse] + part[coarse:]
        pull = (part[:, :coarse] + part[:, coarse:]) * (2.0 * share)
        turned = pltpu.roll(pull, freqs, 1)
        return jnp.concatenate(
            [jnp.where(first_half, pull, turned), jnp.where(first_half, turned, pull)], axis=1
        )

    def backward(c, first, pull):
        keep = c % plan.stores

        def fall(i):
            for k in (2 * i, 2 * i + 1):
                high, low = split(fields[keep, first + k] * (pull * weight[first + k]))
                sums = []
                for h in range(2):
                    left = jnp.concatenate([lane_block(high, h), lane_block(low, h)], axis=1)
                    part = dot(left, tabs["down_cols"][h])
                    sums.append(part[:, :band] + part[:, band:])
                along = shift[1, first + k] + reach
                flip = jnp.where(residue >= along, 1.0, -1.0).astype(f32)
                high, low = split(sums[0] + flip * sums[1])
                lifts[:band, k * band : (k + 1) * band] = high
                lifts[band:, k * band : (k + 1) * band] = low

        def settle(i):
            part = dot(tabs["down_rows"][...], lifts[:, 2 * i * band : 2 * (i + 1) * band])
            part = part[:band] + part[band:]
            for k in range(2):
                s = first + 2 * i + k
                mine = lane_block(part, k)
                mine = (mine[:freqs] + sign * pltpu.roll(mine[freqs:], freqs, 1)) * pupils[s]
                rows = pl.ds(shift[0, s] + reach, freqs)
                near = residue >= shift[1, s] + reach
                zero = jnp.zeros_like(mine)
                grads[c, 0, rows, :] += jnp.where(near, mine, zero)
                grads[c, 1, rows, :] += jnp.where(near, zero, mine)

        skewed([fall, settle], pairs, SKEW)

    copies[2].wait()
    grads[...] = jnp.zeros_like(grads)
    rounds = sources // group
    for c in range(plan.tile_cols):
        power = jnp.zeros((coarse, 2 * coarse), f32)
        if rounds == 1:
            power = forward(c, 0, power)
        else:
            power = lax.fori_loop(0, rounds, lambda g, p: forward(c, g * group, p), power)
        pull = fine(c, power)
        if rounds == 1:
            backward(c, 0, pull)
        else:
            lax.fori_loop(0, rounds, lambda g, n: (backward(c, g * group, pull), n)[1], 0)

    copies[3].wait()
    wide = plan.wide
    bands = jnp.concatenate([grads[c, k] for c in range(plan.tile_cols) for k in range(2)], axis=1) * scale
    high, low = split(bands)
    part = dot(high, final_tab[...])
    part = part[:, : 2 * wide] + part[:, 2 * wide :] + dot(low, final_tab[:, : 2 * wide])
    high, low = split(jnp.concatenate([part[:, :wide], part[:, wide:]], axis=0))
    rows_high, rows_low = tabs["final_rows"][0], tabs["final_rows"][1]
    whole_grad[...] = dot(rows_high, high) + dot(rows_high, low) + dot(rows_low, high)
    own_out[...] = whole_grad[HALO : HALO + TS, : plan.width]
    rim_start = pl.multiple_of(jnp.where(tile_row == 0, HALO + TS, 0), HALO)
    row_out[...] = whole_grad[pl.ds(rim_start, HALO), : plan.width]


def finish_kernel(own, row, out):
    tile_row = lax.axis_index("tile")
    out[...] = own[...]
    first = pl.multiple_of(jnp.where(tile_row == 0, TS - HALO, 0), HALO)
    out[pl.ds(first, HALO), :] += row[...]


def local_image(plan, mask, target, pupil, source_shift, source_weight, halo):
    tables = plan.tables()
    names = tuple(tables)
    vmem = pl.BlockSpec(memory_space=pltpu.VMEM)
    smem = pl.BlockSpec(memory_space=pltpu.SMEM)
    distant = pl.BlockSpec(memory_space=pltpu.MemorySpace.HBM)
    sources, group, tile_cols = plan.sources, plan.group, plan.tile_cols
    band, coarse = plan.band, plan.coarse
    return pl.pallas_call(
        functools.partial(image_kernel, plan, names),
        out_shape=[
            jax.ShapeDtypeStruct((TS, plan.width), f32),
            jax.ShapeDtypeStruct((HALO, plan.width), f32),
        ],
        in_specs=[smem, smem, vmem, distant, distant, vmem]
        + [distant if name in ("e_rim", "final_cols") else vmem for name in names],
        out_specs=[vmem] * 2,
        scratch_shapes=[
            pltpu.VMEM((TS, plan.cols), f32),
            pltpu.VMEM((TS, plan.cols), f32),
            pltpu.VMEM(tables["e_rim"].shape[1:], bf16),
            pltpu.VMEM(tables["final_cols"].shape[1:], bf16),
            pltpu.VMEM((sources, plan.freqs, band), f32),
            pltpu.VMEM((tile_cols, 4, band, band), f32),
            pltpu.VMEM((plan.stores, sources, coarse, 2 * coarse), f32),
            pltpu.VMEM((tile_cols, 2, band, band), f32),
            pltpu.VMEM((PAD, plan.wide), f32),
            pltpu.VMEM((2 * band, plan.cols), bf16),
            pltpu.VMEM((2 * band, plan.cols), bf16),
            pltpu.VMEM((TS, 2 * coarse), bf16),
            pltpu.VMEM((2 * band, group * band), bf16),
            pltpu.VMEM((group, coarse, 2 * band), bf16),
            pltpu.SemaphoreType.DMA((4,)),
        ],
        compiler_params=pltpu.CompilerParams(vmem_limit_bytes=(28 + sources // 8) * 1024 * 1024),
        name="image",
    )(source_shift.T, source_weight, pupil, mask, target, halo, *[jnp.asarray(tables[n]) for n in names])


def shards(plan, mask, target, pupil, source_shift, source_weight):
    tile_row = lax.axis_index("tile")
    swap = [(0, 1), (1, 0)]
    edge = lax.dynamic_slice_in_dim(mask, jnp.where(tile_row == 0, TS - HALO, 0), HALO, 0)
    halo = lax.ppermute(edge, "tile", swap)
    own, row = local_image(plan, mask, target, pupil, source_shift, source_weight, halo)
    row = lax.ppermute(row, "tile", swap)
    vmem = pl.BlockSpec(memory_space=pltpu.VMEM)
    return pl.pallas_call(
        finish_kernel,
        out_shape=jax.ShapeDtypeStruct((TS, plan.width), f32),
        in_specs=[vmem] * 2,
        out_specs=vmem,
        name="finish",
    )(own, row)


def solution(mesh):
    sizes = dict(mesh.shape)

    def run(mask, target, pupil, source_shift, source_weight):
        plan = Plan(pupil.shape[0], mask.shape[1], sizes["src"], source_shift.shape[0])
        placed = (P(("groups", "tile"), None), P(("groups", "tile"), None), P(), P(), P())
        return jax.shard_map(
            functools.partial(shards, plan),
            mesh=mesh,
            in_specs=placed,
            out_specs=P(("groups", "tile"), "src"),
            check_vma=False,
        )(mask, target, pupil, source_shift, source_weight)

    return run
```

profile of v0, /device:TPU:13, one launch (start us, length us, event | category | flops | bytes accessed | tf_op | source)
XLA Modules:
  0.0 43.7 jit_solution(18121377039638405861)
XLA Ops:
  0.0 1.0 %constant_dynamic-slice_fusion = f32[64,1024]{1,0:T(8,128)S(1)} fusion(f32[512,1024]{1,0:T(8,128)} %mask.1, s32[]{:T(128)S(6)} %select_n.5), kind=kLoop, calls=%fused_computation | loop fusion | bytes 524292 | tf_op jit(solution)/shard_map/dynamic_slice | solution.py:408
  1.0 0.7 %collective-permute-start = (f32[64,1024]{1,0:T(8,128)S(1)}, f32[64,1024]{1,0:T(8,128)S(1)}, u32[]{:S(2)}, u32[]{:S(2)}) collective-permute-start(f32[64,1024]{1,0:T(8,128)S(1)} %constant_dynamic-slice_fusion), channel_id=1, source_target_pairs={{0,1},{1,0},{2,3},{3,2},{4,5},{5,4},{6,7},{7,6},{8,9},{9,8},{10,11... | collective-permute-start | bytes 786440 | tf_op jit(solution)/shard_map/ppermute | solution.py:409
  1.7 1.2 %collective-permute-done.halo = f32[64,1024]{1,0:T(8,128)S(1)} collective-permute-done((f32[64,1024]{1,0:T(8,128)S(1)}, f32[64,1024]{1,0:T(8,128)S(1)}, u32[]{:S(2)}, u32[]{:S(2)}) %collective-permute-start) | collective-permute-done | bytes 262176 | tf_op jit(solution)/shard_map/ppermute | solution.py:409
  2.9 0.0 copy-start
  2.9 2.2 %copy-done = bf16[8,512,512]{2,1,0:T(8,128)(2,1)S(1)} copy-done((bf16[8,512,512]{2,1,0:T(8,128)(2,1)S(1)}, bf16[8,512,512]{2,1,0:T(8,128)(2,1)}, u32[]{:S(2)}) %copy-start) | copy-done | bytes 4194328
  5.1 0.0 copy-start.1
  5.1 1.6 %copy-done.1 = f32[512,1024]{1,0:T(8,128)S(1)} copy-done((f32[512,1024]{1,0:T(8,128)S(1)}, f32[512,1024]{1,0:T(8,128)}, u32[]{:S(2)}) %copy-start.1) | copy-done | bytes 2097176
  6.7 0.0 copy-start.2
  6.7 1.6 %copy-done.2 = f32[512,1024]{1,0:T(8,128)S(1)} copy-done((f32[512,1024]{1,0:T(8,128)S(1)}, f32[512,1024]{1,0:T(8,128)}, u32[]{:S(2)}) %copy-start.2) | copy-done | bytes 2097176
  8.2 0.0 copy-start.3
  8.2 1.3 %copy-done.3 = bf16[1280,512]{1,0:T(8,128)(2,1)S(1)} copy-done((bf16[1280,512]{1,0:T(8,128)(2,1)S(1)}, bf16[1280,512]{1,0:T(8,128)(2,1)}, u32[]{:S(2)}) %copy-start.3) | copy-done | bytes 1310744
  9.6 0.0 copy-start.4
  9.6 1.3 %copy-done.4 = bf16[1280,512]{1,0:T(8,128)(2,1)S(1)} copy-done((bf16[1280,512]{1,0:T(8,128)(2,1)S(1)}, bf16[1280,512]{1,0:T(8,128)(2,1)}, u32[]{:S(2)}) %copy-start.4) | copy-done | bytes 1310744
  10.9 0.0 copy-start.5
  10.9 1.1 %copy-done.5 = bf16[2,640,256]{2,1,0:T(8,128)(2,1)S(1)} copy-done((bf16[2,640,256]{2,1,0:T(8,128)(2,1)S(1)}, bf16[2,640,256]{2,1,0:T(8,128)(2,1)}, u32[]{:S(2)}) %copy-start.5) | copy-done | bytes 655384
  12.0 0.0 copy-start.6
  12.0 1.0 %copy-done.6 = bf16[256,1024]{1,0:T(8,128)(2,1)S(1)} copy-done((bf16[256,1024]{1,0:T(8,128)(2,1)S(1)}, bf16[256,1024]{1,0:T(8,128)(2,1)}, u32[]{:S(2)}) %copy-start.6) | copy-done | bytes 524312
  13.0 0.0 copy-start.7
  13.0 1.0 %copy-done.7 = bf16[512,512]{1,0:T(8,128)(2,1)S(1)} copy-done((bf16[512,512]{1,0:T(8,128)(2,1)S(1)}, bf16[512,512]{1,0:T(8,128)(2,1)}, u32[]{:S(2)}) %copy-start.7) | copy-done | bytes 524312
  14.1 0.0 copy-start.8
  14.1 0.9 %copy-done.8 = bf16[256,512]{1,0:T(8,128)(2,1)S(1)} copy-done((bf16[256,512]{1,0:T(8,128)(2,1)S(1)}, bf16[256,512]{1,0:T(8,128)(2,1)}, u32[]{:S(2)}) %copy-start.8) | copy-done | bytes 262168
  15.0 0.0 copy-start.9
  15.0 0.9 %copy-done.9 = bf16[512,256]{1,0:T(8,128)(2,1)S(1)} copy-done((bf16[512,256]{1,0:T(8,128)(2,1)S(1)}, bf16[512,256]{1,0:T(8,128)(2,1)}, u32[]{:S(2)}) %copy-start.9) | copy-done | bytes 262168
  16.0 0.0 copy-start.10
  16.0 0.9 %copy-done.10 = bf16[512,256]{1,0:T(8,128)(2,1)S(1)} copy-done((bf16[512,256]{1,0:T(8,128)(2,1)S(1)}, bf16[512,256]{1,0:T(8,128)(2,1)}, u32[]{:S(2)}) %copy-start.10) | copy-done | bytes 262168
  16.9 0.0 copy-start.11
  16.9 0.9 %copy-done.11 = bf16[2,256,256]{2,1,0:T(8,128)(2,1)S(1)} copy-done((bf16[2,256,256]{2,1,0:T(8,128)(2,1)S(1)}, bf16[2,256,256]{2,1,0:T(8,128)(2,1)}, u32[]{:S(2)}) %copy-start.11) | copy-done | bytes 262168
  17.9 0.0 copy-start.12
  17.9 0.9 %copy-done.12 = bf16[2,256,256]{2,1,0:T(8,128)(2,1)S(1)} copy-done((bf16[2,256,256]{2,1,0:T(8,128)(2,1)S(1)}, bf16[2,256,256]{2,1,0:T(8,128)(2,1)}, u32[]{:S(2)}) %copy-start.12) | copy-done | bytes 262168
  18.8 0.0 copy-start.13
  18.8 0.9 %copy-done.13 = bf16[2,512,64]{2,1,0:T(8,128)(2,1)S(1)} copy-done((bf16[2,512,64]{2,1,0:T(8,128)(2,1)S(1)}, bf16[2,512,64]{2,1,0:T(8,128)(2,1)}, u32[]{:S(2)}) %copy-start.13) | copy-done | bytes 131096
  19.8 0.0 copy-start.15
  19.8 0.9 %copy-done.15 = bf16[256,256]{1,0:T(8,128)(2,1)S(1)} copy-done((bf16[256,256]{1,0:T(8,128)(2,1)S(1)}, bf16[256,256]{1,0:T(8,128)(2,1)}, u32[]{:S(2)}) %copy-start.15) | copy-done | bytes 131096
  20.7 0.0 copy-start.16
  20.7 0.9 %copy-done.16 = bf16[256,256]{1,0:T(8,128)(2,1)S(1)} copy-done((bf16[256,256]{1,0:T(8,128)(2,1)S(1)}, bf16[256,256]{1,0:T(8,128)(2,1)}, u32[]{:S(2)}) %copy-start.16) | copy-done | bytes 131096
  21.6 0.0 copy-start.17
  21.6 0.8 %copy-done.17 = f32[64,64]{1,0:T(8,128)S(1)} copy-done((f32[64,64]{1,0:T(8,128)S(1)}, f32[64,64]{1,0:T(8,128)}, u32[]{:S(2)}) %copy-start.17) | copy-done | bytes 16408
  22.3 0.7 %copy-done.18 = s32[24,2]{0,1:T(2,128)S(1)} copy-done((s32[24,2]{0,1:T(2,128)S(1)}, s32[24,2]{0,1:T(2,128)}, u32[]{:S(2)}) %copy-start.18) | copy-done | bytes 216
  23.0 0.0 copy-start.19
  23.0 0.7 %copy-done.19 = f32[24]{0:T(128)S(1)} copy-done((f32[24]{0:T(128)S(1)}, f32[24]{0:T(128)}, u32[]{:S(2)}) %copy-start.19) | copy-done | bytes 120
  23.7 15.8 %image.1 = (f32[512,128]{1,0:T(8,128)S(1)}, f32[64,128]{1,0:T(8,128)S(1)}) custom-call(s32[2,24]{1,0:T(2,128)S(1)} %bitcast.1, f32[24]{0:T(128)S(1)} %copy-done.19, f32[64,64]{1,0:T(8,128)S(1)} %copy-done.17, f32[512,1024]{1,0:T(8,128)S(1)} %copy-done.1, f32[512,1024]{1,0:T(8,128)S(1)} %copy-done.2, f32[64,1024]{1,0:T(8,128)S(1)} %collective-permute-done.halo, ...), custom_call_target="tpu_custom_call" | custom-call | tf_op jit(solution)/shard_map/image/pallas_call | solution.py:374
  39.4 0.0 copy-start.14
  39.4 0.7 %copy-done.14 = f32[512,128]{1,0:T(8,128)} copy-done((f32[512,128]{1,0:T(8,128)}, f32[512,128]{1,0:T(8,128)S(1)}, u32[]{:S(2)}) %copy-start.14) | copy-done | bytes 262168
  40.1 0.4 collective-permute-start.1
  40.5 0.9 %collective-permute-done.1.row = f32[64,128]{1,0:T(8,128)S(1)} collective-permute-done((f32[64,128]{1,0:T(8,128)S(1)}, f32[64,128]{1,0:T(8,128)S(1)}, u32[]{:S(2)}, u32[]{:S(2)}) %collective-permute-start.1) | collective-permute-done | bytes 32800 | tf_op jit(solution)/shard_map/ppermute | solution.py:411
  41.4 0.0 copy-start.20
  41.4 0.6 %copy-done.20 = f32[64,128]{1,0:T(8,128)} copy-done((f32[64,128]{1,0:T(8,128)}, f32[64,128]{1,0:T(8,128)S(1)}, u32[]{:S(2)}) %copy-start.20) | copy-done | bytes 32792
  42.0 1.7 %finish.1 = f32[512,128]{1,0:T(8,128)} custom-call(f32[512,128]{1,0:T(8,128)} %copy-done.14, f32[64,128]{1,0:T(8,128)} %copy-done.20), custom_call_target="tpu_custom_call" | custom-call | tf_op jit(solution)/shard_map/finish/pallas_call | solution.py:413
  (1 shorter events, 0.0 us)
Async XLA Ops:
  1.0 1.9 %collective-permute-start = (f32[64,1024]{1,0:T(8,128)S(1)}, f32[64,1024]{1,0:T(8,128)S(1)}, u32[]{:S(2)}, u32[]{:S(2)}) collective-permute-start(f32[64,1024]{1,0:T(8,128)S(1)} %constant_dynamic-slice_fusion), channel_id=1, source_target_pairs={{0,1},{1,0},{2,3},{3,2},{4,5},{5,4},{6,7},{7,6},{8,9},{9,8},{10,11... | collective-permute-start | bytes 786440 | tf_op jit(solution)/shard_map/ppermute | solution.py:409
  2.9 2.2 %copy-start = (bf16[8,512,512]{2,1,0:T(8,128)(2,1)S(1)}, bf16[8,512,512]{2,1,0:T(8,128)(2,1)}, u32[]{:S(2)}) copy-start(bf16[8,512,512]{2,1,0:T(8,128)(2,1)} %constant.51.clone.refs_13_) | copy-start | bytes 12582916
  5.1 1.6 %copy-start.1 = (f32[512,1024]{1,0:T(8,128)S(1)}, f32[512,1024]{1,0:T(8,128)}, u32[]{:S(2)}) copy-start(f32[512,1024]{1,0:T(8,128)} %mask.1) | copy-start | bytes 6291460
  6.7 1.6 %copy-start.2 = (f32[512,1024]{1,0:T(8,128)S(1)}, f32[512,1024]{1,0:T(8,128)}, u32[]{:S(2)}) copy-start(f32[512,1024]{1,0:T(8,128)} %target.1) | copy-start | bytes 6291460
  8.2 1.3 %copy-start.3 = (bf16[1280,512]{1,0:T(8,128)(2,1)S(1)}, bf16[1280,512]{1,0:T(8,128)(2,1)}, u32[]{:S(2)}) copy-start(bf16[1280,512]{1,0:T(8,128)(2,1)} %constant.42.clone.refs_4_) | copy-start | bytes 3932164
  9.6 1.3 %copy-start.4 = (bf16[1280,512]{1,0:T(8,128)(2,1)S(1)}, bf16[1280,512]{1,0:T(8,128)(2,1)}, u32[]{:S(2)}) copy-start(bf16[1280,512]{1,0:T(8,128)(2,1)} %constant.41.clone.refs_3_) | copy-start | bytes 3932164
  10.9 1.1 %copy-start.5 = (bf16[2,640,256]{2,1,0:T(8,128)(2,1)S(1)}, bf16[2,640,256]{2,1,0:T(8,128)(2,1)}, u32[]{:S(2)}) copy-start(bf16[2,640,256]{2,1,0:T(8,128)(2,1)} %constant.40.clone.refs_2_) | copy-start | bytes 1966084
  12.0 1.0 %copy-start.6 = (bf16[256,1024]{1,0:T(8,128)(2,1)S(1)}, bf16[256,1024]{1,0:T(8,128)(2,1)}, u32[]{:S(2)}) copy-start(bf16[256,1024]{1,0:T(8,128)(2,1)} %constant.49.clone.refs_11_) | copy-start | bytes 1572868
  13.0 1.0 %copy-start.7 = (bf16[512,512]{1,0:T(8,128)(2,1)S(1)}, bf16[512,512]{1,0:T(8,128)(2,1)}, u32[]{:S(2)}) copy-start(bf16[512,512]{1,0:T(8,128)(2,1)} %constant.38.clone.refs_0_) | copy-start | bytes 1572868
  14.1 0.9 %copy-start.8 = (bf16[256,512]{1,0:T(8,128)(2,1)S(1)}, bf16[256,512]{1,0:T(8,128)(2,1)}, u32[]{:S(2)}) copy-start(bf16[256,512]{1,0:T(8,128)(2,1)} %constant.50.clone.refs_12_) | copy-start | bytes 786436
  15.0 0.9 %copy-start.9 = (bf16[512,256]{1,0:T(8,128)(2,1)S(1)}, bf16[512,256]{1,0:T(8,128)(2,1)}, u32[]{:S(2)}) copy-start(bf16[512,256]{1,0:T(8,128)(2,1)} %constant.48.clone.refs_10_) | copy-start | bytes 786436
  16.0 0.9 %copy-start.10 = (bf16[512,256]{1,0:T(8,128)(2,1)S(1)}, bf16[512,256]{1,0:T(8,128)(2,1)}, u32[]{:S(2)}) copy-start(bf16[512,256]{1,0:T(8,128)(2,1)} %constant.47.clone.refs_9_) | copy-start | bytes 786436
  16.9 0.9 %copy-start.11 = (bf16[2,256,256]{2,1,0:T(8,128)(2,1)S(1)}, bf16[2,256,256]{2,1,0:T(8,128)(2,1)}, u32[]{:S(2)}) copy-start(bf16[2,256,256]{2,1,0:T(8,128)(2,1)} %constant.46.clone.refs_8_) | copy-start | bytes 786436
  17.9 0.9 %copy-start.12 = (bf16[2,256,256]{2,1,0:T(8,128)(2,1)S(1)}, bf16[2,256,256]{2,1,0:T(8,128)(2,1)}, u32[]{:S(2)}) copy-start(bf16[2,256,256]{2,1,0:T(8,128)(2,1)} %constant.45.clone.refs_7_) | copy-start | bytes 786436
  18.8 0.9 %copy-start.13 = (bf16[2,512,64]{2,1,0:T(8,128)(2,1)S(1)}, bf16[2,512,64]{2,1,0:T(8,128)(2,1)}, u32[]{:S(2)}) copy-start(bf16[2,512,64]{2,1,0:T(8,128)(2,1)} %constant.39.clone.refs_1_) | copy-start | bytes 393220
  19.8 0.9 %copy-start.15 = (bf16[256,256]{1,0:T(8,128)(2,1)S(1)}, bf16[256,256]{1,0:T(8,128)(2,1)}, u32[]{:S(2)}) copy-start(bf16[256,256]{1,0:T(8,128)(2,1)} %constant.44.clone.refs_6_) | copy-start | bytes 393220
  20.7 0.9 %copy-start.16 = (bf16[256,256]{1,0:T(8,128)(2,1)S(1)}, bf16[256,256]{1,0:T(8,128)(2,1)}, u32[]{:S(2)}) copy-start(bf16[256,256]{1,0:T(8,128)(2,1)} %constant.43.clone.refs_5_) | copy-start | bytes 393220
  21.6 0.8 %copy-start.17 = (f32[64,64]{1,0:T(8,128)S(1)}, f32[64,64]{1,0:T(8,128)}, u32[]{:S(2)}) copy-start(f32[64,64]{1,0:T(8,128)} %pupil.1) | copy-start | bytes 49156
  22.3 0.7 %copy-start.18 = (s32[24,2]{0,1:T(2,128)S(1)}, s32[24,2]{0,1:T(2,128)}, u32[]{:S(2)}) copy-start(s32[24,2]{0,1:T(2,128)} %param.22) | copy-start | bytes 580
  23.0 0.7 %copy-start.19 = (f32[24]{0:T(128)S(1)}, f32[24]{0:T(128)}, u32[]{:S(2)}) copy-start(f32[24]{0:T(128)} %weight.1) | copy-start | bytes 292
  39.4 0.7 %copy-start.14 = (f32[512,128]{1,0:T(8,128)}, f32[512,128]{1,0:T(8,128)S(1)}, u32[]{:S(2)}) copy-start(f32[512,128]{1,0:T(8,128)S(1)} %get-tuple-element.7.own) | copy-start | bytes 786436
  40.1 1.2 %collective-permute-start.1 = (f32[64,128]{1,0:T(8,128)S(1)}, f32[64,128]{1,0:T(8,128)S(1)}, u32[]{:S(2)}, u32[]{:S(2)}) collective-permute-start(f32[64,128]{1,0:T(8,128)S(1)} %get-tuple-element.8), channel_id=1, source_target_pairs={{0,1},{1,0},{2,3},{3,2},{4,5},{5,4},{6,7},{7,6},{8,9},{9,8},{10,11... | collective-permute-start | bytes 98312 | tf_op jit(solution)/shard_map/ppermute | solution.py:411
  41.4 0.6 %copy-start.20 = (f32[64,128]{1,0:T(8,128)}, f32[64,128]{1,0:T(8,128)S(1)}, u32[]{:S(2)}) copy-start(f32[64,128]{1,0:T(8,128)S(1)} %collective-permute-done.1.row) | copy-start | bytes 98308
where the time goes:
time: 44.4 us; the launch traced here: 43.7 us
  local copies, waits for them, and re-layouts  23 us (52%)
  Pallas kernels  17.4 us (39%)
  waiting for transfers between devices  2.02 us (5%)
  starting transfers between devices  1.12 us (3%)
    unnamed x42, local copies, waits for them, and re-layouts  22.1 us
    pallas_call x1, Pallas kernels, local_image(): pl.pallas_call(functools.partial(image_kernel, plan, names), out_shape=[j...  15.8 us
    pallas_call x1, Pallas kernels, shards(): pl.pallas_call(finish_kernel, out_shape=jax.ShapeDtypeStruct((TS, plan.wi...  1.68 us
    ppermute x1, waiting for transfers between devices, shards(): halo = lax.ppermute(edge, 'tile', swap)  1.16 us
    dynamic_slice x1, local copies, waits for them, and re-layouts, shards(): lax.dynamic_slice_in_dim(mask, jnp.where(tile_row == 0, TS - HALO, 0), HA...  0.97 us
  transfers between devices with their start and end apart: 2, of which 2 were waited for; matrix products, arithmetic and copies ran while one was open for 0% of the time, Pallas kernels for 0%

commit v1 on v0

--- a/solution.py
+++ b/solution.py
@@ -149,25 +149,33 @@
                 stage(step - late * gap)
 
 
-def image_kernel(plan, names, shift, weight, pupil, mask, target, halo, *refs):
-    tabs = dict(zip(names, refs[: len(names)]))
+def image_kernel(plan, names, shift, weight, *refs):
+    far = dict(zip(names, refs[: len(names)]))
     own_out, row_out = refs[len(names) : len(names) + 2]
+    near = dict(zip(names, refs[len(names) + 2 :]))
     (
-        mask_v, target_v, e_rim, final_tab, pupils, spectrum, fields, grads, whole_grad,
-        u_high, u_low, woven, lifts, lines, sems,
-    ) = refs[len(names) + 2 :]
+        pupils, spectrum, fields, grads, whole_grad, u_high, u_low, woven, lifts, lines, sems,
+    ) = refs[2 * len(names) + 2 :]
     sources, group = plan.sources, plan.group
     freqs, reach, band, coarse = plan.freqs, plan.reach, plan.band, plan.coarse
     tile_row = lax.axis_index("tile")
     block = lax.axis_index("src")
-    copies = [
-        pltpu.make_async_copy(mask, mask_v, sems.at[0]),
-        pltpu.make_async_copy(tabs["e_rim"].at[tile_row], e_rim, sems.at[1]),
-        pltpu.make_async_copy(target, target_v, sems.at[2]),
-        pltpu.make_async_copy(tabs["final_cols"].at[block], final_tab, sems.at[3]),
-    ]
-    for copy in copies:
-        copy.start()
+    picked = {"e_rim": tile_row, "final_cols": block}
+    pending = {}
+    for i, name in enumerate(names):
+        source = far[name].at[picked[name]] if name in picked else far[name]
+        pending[name] = pltpu.make_async_copy(source, near[name], sems.at[i])
+        pending[name].start()
+
+    def need(*wanted):
+        for name in wanted:
+            if name in pending:
+                pending.pop(name).wait()
+
+    tabs = near
+    mask_v, target_v, e_rim, final_tab, halo = (
+        near[name] for name in ("mask", "target", "e_rim", "final_cols", "halo")
+    )
     total = weight[0]
     for s in range(1, sources):
         total = total + weight[s]
@@ -176,7 +184,8 @@
     first_half = lane < freqs
     residue = jnp.where(first_half, lane, lane - freqs)
     sign = jnp.where(first_half, 1.0, -1.0).astype(f32)
-    doubled = jnp.concatenate([pupil[...], pupil[...]], axis=1)
+    need("pupil")
+    doubled = jnp.concatenate([near["pupil"][...]] * 2, axis=1)
 
     def place_pupil(s):
         pupils[s] = pltpu.roll(doubled, shift[1, s] + reach, 1)
@@ -187,8 +196,7 @@
     else:
         lax.fori_loop(0, sources, lambda s, c: (place_pupil(s), c)[1], 0)
 
-    copies[0].wait()
-    copies[1].wait()
+    need("mask", "e_own", "e_rim", "halo")
     e_own, rim_table = tabs["e_own"], e_rim[...]
     for n in range(0, plan.cols, 256):
         high, low = split(mask_v[:, n : n + 256])
@@ -201,6 +209,7 @@
         u_low[:, n : n + 256] = low
     scale = 1.0 / (PAD * PAD)
     for c, (first, last) in enumerate(plan.spans):
+        need(f"col{c}")
         high = jnp.concatenate([u_high[:band, first:last], u_high[band:, first:last]], axis=1)
         low = jnp.concatenate([u_low[:band, first:last], u_low[band:, first:last]], axis=1)
         prod = dot(high, tabs[f"col{c}"][...])
@@ -327,7 +336,7 @@
 
         skewed([fall, settle], pairs, SKEW)
 
-    copies[2].wait()
+    need("up_rows", "up_cols")
     grads[...] = jnp.zeros_like(grads)
     rounds = sources // group
     for c in range(plan.tile_cols):
@@ -336,13 +345,15 @@
             power = forward(c, 0, power)
         else:
             power = lax.fori_loop(0, rounds, lambda g, p: forward(c, g * group, p), power)
+        need("target", "weave_rows", "weave_up", "weave_cols", "weave_down")
         pull = fine(c, power)
+        need("down_rows", "down_cols")
         if rounds == 1:
             backward(c, 0, pull)
         else:
             lax.fori_loop(0, rounds, lambda g, n: (backward(c, g * group, pull), n)[1], 0)
 
-    copies[3].wait()
+    need("final_cols", "final_rows")
     wide = plan.wide
     bands = jnp.concatenate([grads[c, k] for c in range(plan.tile_cols) for k in range(2)], axis=1) * scale
     high, low = split(bands)
@@ -350,23 +361,44 @@
     part = part[:, : 2 * wide] + part[:, 2 * wide :] + dot(low, final_tab[:, : 2 * wide])
     high, low = split(jnp.concatenate([part[:, :wide], part[:, wide:]], axis=0))
     rows_high, rows_low = tabs["final_rows"][0], tabs["final_rows"][1]
-    whole_grad[...] = dot(rows_high, high) + dot(rows_high, low) + dot(rows_low, high)
-    own_out[...] = whole_grad[HALO : HALO + TS, : plan.width]
+    final = dot(rows_high, high) + dot(rows_high, low) + dot(rows_low, high)
+    whole_grad[...] = final[:, : plan.width]
     rim_start = pl.multiple_of(jnp.where(tile_row == 0, HALO + TS, 0), HALO)
-    row_out[...] = whole_grad[pl.ds(rim_start, HALO), : plan.width]
-
-
-def finish_kernel(own, row, out):
+    ends = [
+        pltpu.make_async_copy(whole_grad.at[pl.ds(rim_start, HALO)], row_out, sems.at[0]),
+        pltpu.make_async_copy(whole_grad.at[pl.ds(HALO, TS)], own_out, sems.at[1]),
+    ]
+    for end in ends:
+        end.start()
+    for end in ends:
+        end.wait()
+
+
+def finish_kernel(own, row, out, mine, other, sems):
     tile_row = lax.axis_index("tile")
-    out[...] = own[...]
     first = pl.multiple_of(jnp.where(tile_row == 0, TS - HALO, 0), HALO)
-    out[pl.ds(first, HALO), :] += row[...]
+    rows = pl.ds(first, HALO)
+    loads = [
+        pltpu.make_async_copy(out.at[rows], mine, sems.at[0]),
+        pltpu.make_async_copy(row, other, sems.at[1]),
+    ]
+    for load in loads:
+        load.start()
+    for load in loads:
+        load.wait()
+    mine[...] = mine[...] + other[...]
+    store = pltpu.make_async_copy(mine, out.at[rows], sems.at[0])
+    store.start()
+    store.wait()
 
 
 def local_image(plan, mask, target, pupil, source_shift, source_weight, halo):
     tables = plan.tables()
-    names = tuple(tables)
-    vmem = pl.BlockSpec(memory_space=pltpu.VMEM)
+    arrays = {"mask": mask, "e_own": tables["e_own"], "e_rim": tables["e_rim"], "pupil": pupil}
+    arrays.update(halo=halo, **{n: t for n, t in tables.items() if n not in arrays}, target=target)
+    names = tuple(arrays)
+    picked = ("e_rim", "final_cols")
+    local = {n: a.shape[1:] if n in picked else a.shape for n, a in arrays.items()}
     smem = pl.BlockSpec(memory_space=pltpu.SMEM)
     distant = pl.BlockSpec(memory_space=pltpu.MemorySpace.HBM)
     sources, group, tile_cols = plan.sources, plan.group, plan.tile_cols
@@ -377,29 +409,25 @@
             jax.ShapeDtypeStruct((TS, plan.width), f32),
             jax.ShapeDtypeStruct((HALO, plan.width), f32),
         ],
-        in_specs=[smem, smem, vmem, distant, distant, vmem]
-        + [distant if name in ("e_rim", "final_cols") else vmem for name in names],
-        out_specs=[vmem] * 2,
-        scratch_shapes=[
-            pltpu.VMEM((TS, plan.cols), f32),
-            pltpu.VMEM((TS, plan.cols), f32),
-            pltpu.VMEM(tables["e_rim"].shape[1:], bf16),
-            pltpu.VMEM(tables["final_cols"].shape[1:], bf16),
+        in_specs=[smem, smem] + [distant] * len(names),
+        out_specs=[distant] * 2,
+        scratch_shapes=[pltpu.VMEM(local[n], arrays[n].dtype) for n in names]
+        + [
             pltpu.VMEM((sources, plan.freqs, band), f32),
             pltpu.VMEM((tile_cols, 4, band, band), f32),
             pltpu.VMEM((plan.stores, sources, coarse, 2 * coarse), f32),
             pltpu.VMEM((tile_cols, 2, band, band), f32),
-            pltpu.VMEM((PAD, plan.wide), f32),
+            pltpu.VMEM((PAD, plan.width), f32),
             pltpu.VMEM((2 * band, plan.cols), bf16),
             pltpu.VMEM((2 * band, plan.cols), bf16),
             pltpu.VMEM((TS, 2 * coarse), bf16),
             pltpu.VMEM((2 * band, group * band), bf16),
             pltpu.VMEM((group, coarse, 2 * band), bf16),
-            pltpu.SemaphoreType.DMA((4,)),
+            pltpu.SemaphoreType.DMA((len(names),)),
         ],
-        compiler_params=pltpu.CompilerParams(vmem_limit_bytes=(28 + sources // 8) * 1024 * 1024),
+        compiler_params=pltpu.CompilerParams(vmem_limit_bytes=60 * 1024 * 1024),
         name="image",
-    )(source_shift.T, source_weight, pupil, mask, target, halo, *[jnp.asarray(tables[n]) for n in names])
+    )(source_shift.T, source_weight, *[jnp.asarray(arrays[n]) for n in names])
 
 
 def shards(plan, mask, target, pupil, source_shift, source_weight):
@@ -409,12 +437,15 @@
     halo = lax.ppermute(edge, "tile", swap)
     own, row = local_image(plan, mask, target, pupil, source_shift, source_weight, halo)
     row = lax.ppermute(row, "tile", swap)
-    vmem = pl.BlockSpec(memory_space=pltpu.VMEM)
+    distant = pl.BlockSpec(memory_space=pltpu.MemorySpace.HBM)
+    piece = pltpu.VMEM((HALO, plan.width), f32)
     return pl.pallas_call(
         finish_kernel,
         out_shape=jax.ShapeDtypeStruct((TS, plan.width), f32),
-        in_specs=[vmem] * 2,
-        out_specs=vmem,
+        in_specs=[distant, pl.BlockSpec(memory_space=pl.ANY)],
+        out_specs=distant,
+        scratch_shapes=[piece, piece, pltpu.SemaphoreType.DMA((2,))],
+        input_output_aliases={0: 0},
         name="finish",
     )(own, row)
 

time: 44.4 us -> 25.1 us (0.57); the launches traced: 43.7 us -> 24.9 us
  local copies, waits for them, and re-layouts: 23 us -> 2.26 us
  Pallas kernels: 17.4 us -> 19.2 us
    unnamed x42 -> x4, local copies, waits for them, and re-layouts: 22.1 us -> 1.3 us
    pallas_call x1, Pallas kernels: 15.8 us -> 17.8 us  [local_image(): pl.pallas_call(functools.partial(image_kernel, plan, names), out_shape=[j...]
where the time goes in v1:
time: 25.1 us; the launch traced here: 24.9 us
  Pallas kernels  19.2 us (76%)
  local copies, waits for them, and re-layouts  2.26 us (9%)
  waiting for transfers between devices  2.23 us (9%)
  starting transfers between devices  1.19 us (5%)
    pallas_call x1, Pallas kernels, local_image(): pl.pallas_call(functools.partial(image_kernel, plan, names), out_shape=[j...  17.8 us
    pallas_call x1, Pallas kernels, shards(): pl.pallas_call(finish_kernel, out_shape=jax.ShapeDtypeStruct((TS, plan.wi...  1.41 us
    unnamed x4, local copies, waits for them, and re-layouts  1.3 us
    ppermute x1, waiting for transfers between devices, shards(): halo = lax.ppermute(edge, 'tile', swap)  1.16 us
    ppermute x1, waiting for transfers between devices, shards(): row = lax.ppermute(row, 'tile', swap)  1.07 us
    dynamic_slice x1, local copies, waits for them, and re-layouts, shards(): lax.dynamic_slice_in_dim(mask, jnp.where(tile_row == 0, TS - HALO, 0), HA...  0.97 us
    ppermute x1, starting transfers between devices, shards(): halo = lax.ppermute(edge, 'tile', swap)  0.74 us
  transfers between devices with their start and end apart: 2, of which 2 were waited for; matrix products, arithmetic and copies ran while one was open for 0% of the time, Pallas kernels for 0%

profile of v1, /device:TPU:13, one launch (start us, length us, event | category | flops | bytes accessed | tf_op | source)
XLA Modules:
  0.0 24.9 jit_solution(10270440074521092298)
XLA Ops:
  0.0 1.0 %constant_dynamic-slice_fusion = f32[64,1024]{1,0:T(8,128)S(1)} fusion(f32[512,1024]{1,0:T(8,128)} %refs_0_.1, s32[]{:T(128)S(6)} %select_n.5), kind=kLoop, calls=%fused_computation | loop fusion | bytes 524292 | tf_op jit(solution)/shard_map/dynamic_slice | solution.py:436
  1.0 0.7 %collective-permute-start = (f32[64,1024]{1,0:T(8,128)S(1)}, f32[64,1024]{1,0:T(8,128)S(1)}, u32[]{:S(2)}, u32[]{:S(2)}) collective-permute-start(f32[64,1024]{1,0:T(8,128)S(1)} %constant_dynamic-slice_fusion), channel_id=1, source_target_pairs={{0,1},{1,0},{2,3},{3,2},{4,5},{5,4},{6,7},{7,6},{8,9},{9,8},{10,11... | collective-permute-start | bytes 786440 | tf_op jit(solution)/shard_map/ppermute | solution.py:437
  1.7 1.2 %collective-permute-done.refs_4_ = f32[64,1024]{1,0:T(8,128)S(1)} collective-permute-done((f32[64,1024]{1,0:T(8,128)S(1)}, f32[64,1024]{1,0:T(8,128)S(1)}, u32[]{:S(2)}, u32[]{:S(2)}) %collective-permute-start) | collective-permute-done | bytes 262176 | tf_op jit(solution)/shard_map/ppermute | solution.py:437
  2.9 0.0 copy-start
  2.9 0.7 %copy-done = f32[64,1024]{1,0:T(8,128)} copy-done((f32[64,1024]{1,0:T(8,128)}, f32[64,1024]{1,0:T(8,128)S(1)}, u32[]{:S(2)}) %copy-start) | copy-done | bytes 262168
  3.6 17.8 %image.1 = (f32[512,128]{1,0:T(8,128)}, f32[64,128]{1,0:T(8,128)}) custom-call(s32[2,24]{1,0:T(2,128)} %bitcast.1, f32[24]{0:T(128)} %weight.1, f32[512,1024]{1,0:T(8,128)} %refs_0_.1, bf16[512,512]{1,0:T(8,128)(2,1)} %constant.38.clone.refs_1_, bf16[2,512,64]{2,1,0:T(8,128)(2,1)} %constant.39.clone.refs_2_, f32[64,64]{1,0:T(8,128)} %refs_3_.1, ...), custom_call_target="tpu_custom_call" | custom-call | tf_op jit(solution)/shard_map/image/pallas_call | solution.py:406
  21.4 0.4 %collective-permute-start.1 = (f32[64,128]{1,0:T(8,128)}, f32[64,128]{1,0:T(8,128)S(1)}, u32[]{:S(2)}, u32[]{:S(2)}) collective-permute-start(f32[64,128]{1,0:T(8,128)} %get-tuple-element.8), channel_id=1, source_target_pairs={{0,1},{1,0},{2,3},{3,2},{4,5},{5,4},{6,7},{7,6},{8,9},{9,8},{10,11... | collective-permute-start | bytes 98312 | tf_op jit(solution)/shard_map/ppermute | solution.py:439
  21.8 1.1 %collective-permute-done.1.row = f32[64,128]{1,0:T(8,128)S(1)} collective-permute-done((f32[64,128]{1,0:T(8,128)}, f32[64,128]{1,0:T(8,128)S(1)}, u32[]{:S(2)}, u32[]{:S(2)}) %collective-permute-start.1) | collective-permute-done | bytes 32800 | tf_op jit(solution)/shard_map/ppermute | solution.py:439
  22.9 0.0 copy-start.1
  22.9 0.6 %copy-done.1 = f32[64,128]{1,0:T(8,128)} copy-done((f32[64,128]{1,0:T(8,128)}, f32[64,128]{1,0:T(8,128)S(1)}, u32[]{:S(2)}) %copy-start.1) | copy-done | bytes 32792
  23.5 1.4 %finish.1 = f32[512,128]{1,0:T(8,128)} custom-call(f32[512,128]{1,0:T(8,128)} %get-tuple-element.7.own, f32[64,128]{1,0:T(8,128)} %copy-done.1), custom_call_target="tpu_custom_call", output_to_operand_aliasing={{}: (0, {})} | custom-call | tf_op jit(solution)/shard_map/finish/pallas_call | solution.py:442
Async XLA Ops:
  1.0 1.9 %collective-permute-start = (f32[64,1024]{1,0:T(8,128)S(1)}, f32[64,1024]{1,0:T(8,128)S(1)}, u32[]{:S(2)}, u32[]{:S(2)}) collective-permute-start(f32[64,1024]{1,0:T(8,128)S(1)} %constant_dynamic-slice_fusion), channel_id=1, source_target_pairs={{0,1},{1,0},{2,3},{3,2},{4,5},{5,4},{6,7},{7,6},{8,9},{9,8},{10,11... | collective-permute-start | bytes 786440 | tf_op jit(solution)/shard_map/ppermute | solution.py:437
  2.9 0.7 %copy-start = (f32[64,1024]{1,0:T(8,128)}, f32[64,1024]{1,0:T(8,128)S(1)}, u32[]{:S(2)}) copy-start(f32[64,1024]{1,0:T(8,128)S(1)} %collective-permute-done.refs_4_) | copy-start | bytes 786436
  21.4 1.5 %collective-permute-start.1 = (f32[64,128]{1,0:T(8,128)}, f32[64,128]{1,0:T(8,128)S(1)}, u32[]{:S(2)}, u32[]{:S(2)}) collective-permute-start(f32[64,128]{1,0:T(8,128)} %get-tuple-element.8), channel_id=1, source_target_pairs={{0,1},{1,0},{2,3},{3,2},{4,5},{5,4},{6,7},{7,6},{8,9},{9,8},{10,11... | collective-permute-start | bytes 98312 | tf_op jit(solution)/shard_map/ppermute | solution.py:439
  22.9 0.6 %copy-start.1 = (f32[64,128]{1,0:T(8,128)}, f32[64,128]{1,0:T(8,128)S(1)}, u32[]{:S(2)}) copy-start(f32[64,128]{1,0:T(8,128)S(1)} %collective-permute-done.1.row) | copy-start | bytes 98308

commit v2 on v1

v2 whole, which is shorter than its diff:
```python
import functools
import math

import jax
import jax.numpy as jnp
import ml_dtypes
import numpy as np
from jax import lax
from jax.experimental import pallas as pl
from jax.experimental.pallas import tpu as pltpu
from jax.sharding import PartitionSpec as P

TS = 512
HALO = 64
PAD = TS + 2 * HALO
LANES = 128
FINE = 256
CHUNK = 1024
LAG = 1
MOST = 24

resist_gain = 25.0
resist_level = 0.25

f32 = jnp.float32
bf16 = jnp.bfloat16


def halves(table):
    table = np.asarray(table, np.float64)
    high = table.astype(np.float32).astype(ml_dtypes.bfloat16)
    low = (table - high.astype(np.float64)).astype(np.float32).astype(ml_dtypes.bfloat16)
    return high, low


def turns(left, right, period):
    angle = 2.0 * np.pi * np.mod(np.outer(left, right), period) / period
    return np.cos(angle), np.sin(angle)


def both(table, axis):
    return np.concatenate(halves(table), axis=axis)


def split(value):
    high = value.astype(bf16)
    return high, (value - high.astype(f32)).astype(bf16)


def dot(left, right):
    return lax.dot_general(left, right, (((1,), (0,)), ((), ())), preferred_element_type=f32)


class Plan:
    def __init__(self, freqs, cols, n_src, sources):
        self.freqs = freqs
        self.reach = (3 * freqs) // 8
        self.band = 2 * freqs
        self.coarse = 2 * freqs
        self.cols = cols
        self.tile_cols = cols // TS
        self.width = cols // n_src
        self.wide = -(-self.width // LANES) * LANES
        self.n_src = n_src
        self.sources = sources
        self.group = max(n for n in range(2, MOST + 1, 2) if sources % n == 0)
        self.stores = self.tile_cols if sources <= MOST else 1
        self.spans = [
            (max(0, c * TS - LANES), min(cols, (c + 1) * TS + LANES)) for c in range(self.tile_cols)
        ]

    def tables(self):
        freqs, band, coarse = self.freqs, self.band, self.coarse
        index = np.arange(band)
        used = (index < freqs + 2 * self.reach).astype(np.float64)
        centre = index - (freqs // 2 + self.reach)
        out = {}
        cosine, sine = turns(centre, np.arange(PAD), PAD)
        rows = np.concatenate([cosine, -sine], axis=0) * np.concatenate([used, used])[:, None]
        out["e_own"] = both(rows[:, HALO : HALO + TS], 0)
        rims = []
        for rim in (rows[:, HALO + TS :], rows[:, :HALO]):
            high, low = halves(rim)
            rims.append(np.concatenate([high, low, high], axis=1))
        out["e_rim"] = np.stack(rims)

        def fold(real, imag):
            return np.concatenate(
                [real[:, :freqs], imag[:, :freqs], real[:, freqs:], imag[:, freqs:]], axis=1
            )

        place = np.arange(-LANES, TS + LANES) + HALO
        inside = ((place >= 0) & (place < PAD)).astype(np.float64)[:, None] * used
        cosine, sine = turns(place, centre, PAD)
        out["cols"] = both(fold(cosine * inside, -sine * inside), 1)
        relative = np.arange(freqs) - freqs // 2
        points = np.arange(coarse)
        cosine, sine = turns(points, relative, coarse)
        high, low = halves(np.concatenate([cosine, -sine], axis=1))
        out["up_rows"] = np.concatenate(
            [np.concatenate([high, high], axis=1), np.concatenate([low, low], axis=1)], axis=0
        )
        high, low = halves(np.concatenate([cosine.T, sine.T], axis=0))
        out["down_rows"] = np.concatenate(
            [np.concatenate([high, high], axis=1), np.concatenate([low, low], axis=1)], axis=0
        )
        order = np.concatenate([points[::2], points[1::2]])
        up, down = [], []
        for some in (points[::2], points[1::2]):
            cosine, sine = turns(centre[:freqs], some, coarse)
            table = np.concatenate(
                [np.concatenate([cosine, sine], axis=1), np.concatenate([-sine, cosine], axis=1)], axis=0
            )
            for into, piece in ((up, table), (down, table.T)):
                pair = both(piece, 1)
                into.append(np.concatenate([pair, pair], axis=0))
        out["up_cols"], out["down_cols"] = np.stack(up), np.stack(down)
        spread = (np.arange(TS) + HALO)[:, None] - (PAD // coarse) * points[None, :]
        weave = np.ones(spread.shape)
        for p in range(1, freqs):
            weave = weave + 2.0 * np.cos(2.0 * np.pi * np.mod(p * spread, PAD) / PAD)
        weave = weave / coarse
        out["weave_rows"] = both(weave, 1)
        out["weave_cols"] = both(weave[:, order], 1)
        turned = both(weave[:, order].T, 1)
        out["weave_up"] = np.concatenate([turned, turned], axis=0)
        out["weave_down"] = both(weave.T, 0)
        blocks = []
        for j in range(self.n_src):
            pieces = []
            for c in range(self.tile_cols):
                place = np.arange(j * self.width, (j + 1) * self.width) - c * TS + HALO
                inside = ((place >= 0) & (place < PAD)).astype(np.float64)[:, None] * used
                cosine = np.zeros((self.wide, band))
                sine = np.zeros((self.wide, band))
                cosine[: self.width], sine[: self.width] = turns(place, centre, PAD)
                cosine[: self.width] *= inside
                sine[: self.width] *= inside
                pieces.append(
                    np.concatenate([fold(cosine, -sine), fold(sine, cosine)], axis=0).T
                )
            blocks.append(both(np.concatenate(pieces, axis=0), 1))
        out["final_cols"] = np.stack(blocks)
        out["final_rows"] = np.stack(halves(rows.T))
        return {name: np.ascontiguousarray(value) for name, value in out.items()}


def merged(*lists):
    keyed = [((i + 0.5) / len(steps), n, step) for n, steps in enumerate(lists) for i, step in enumerate(steps)]
    return [step for _, _, step in sorted(keyed, key=lambda item: item[:2])]


def run(steps):
    for step in steps:
        step()


def image_kernel(plan, names, shift, weight, *refs):
    far = dict(zip(names, refs[: len(names)]))
    own_out, row_out = refs[len(names) : len(names) + 2]
    near = dict(zip(names, refs[len(names) + 2 :]))
    (
        pupils, spectrum, fields, grads, whole_grad, u_high, u_low, woven, lifts, lines, sems,
    ) = refs[2 * len(names) + 2 :]
    sources, group = plan.sources, plan.group
    freqs, reach, band, coarse = plan.freqs, plan.reach, plan.band, plan.coarse
    tile_row = lax.axis_index("tile")
    block = lax.axis_index("src")
    picked = {"e_rim": tile_row, "final_cols": block}
    pending = {}
    for i, name in enumerate(names):
        source = far[name].at[picked[name]] if name in picked else far[name]
        if name.startswith("mask"):
            source = far[name].at[:, pl.ds(int(name[4:]) * CHUNK, CHUNK)]
        pending[name] = pltpu.make_async_copy(source, near[name], sems.at[i])
    early = ("pupil", "e_own", "e_rim", "halo", "cols")
    started = [name for name in names if name in early or name.startswith("mask")]
    for name in started:
        pending[name].start()

    def need(*wanted):
        for name in wanted:
            if name in pending:
                pending.pop(name).wait()

    tabs = near
    target_v, e_rim, final_tab, halo = (
        near[name] for name in ("target", "e_rim", "final_cols", "halo")
    )
    total = weight[0]
    for s in range(1, sources):
        total = total + weight[s]
    scale = 1.0 / (PAD * PAD)
    lane = lax.broadcasted_iota(jnp.int32, (1, band), 1)
    first_half = lane < freqs
    residue = jnp.where(first_half, lane, lane - freqs)
    sign = jnp.where(first_half, 1.0, -1.0).astype(f32)
    need("pupil")
    doubled = jnp.concatenate([near["pupil"][...]] * 2, axis=1)

    def place_pupil(s):
        strength = jnp.sqrt(jnp.full((1, band), weight[s] / total, f32)) * scale
        pupils[s] = pltpu.roll(doubled, shift[1, s] + reach, 1) * strength

    if sources <= MOST:
        for s in range(sources):
            place_pupil(s)
    else:
        lax.fori_loop(0, sources, lambda s, c: (place_pupil(s), c)[1], 0)

    need("e_own", "e_rim", "halo")
    e_own, rim_table = tabs["e_own"], e_rim[...]
    for i in range(0, plan.cols // CHUNK):
        cols = slice(i * CHUNK, (i + 1) * CHUNK)
        need(f"mask{i}")
        if i == 0:
            for name in names:
                if name not in started:
                    pending[name].start()
        high, low = split(near[f"mask{i}"][...])
        rim_high, rim_low = split(halo[:, cols])
        rows = dot(rim_table, jnp.concatenate([rim_high, rim_high, rim_low], axis=0))
        part = dot(e_own[...], high)
        rows = rows + part[: 2 * band] + part[2 * band :] + dot(e_own[: 2 * band, :], low)
        high, low = split(rows)
        u_high[:, cols] = high
        u_low[:, cols] = low
    need("cols")

    def transform(c):
        first, last = plan.spans[c]
        inside = slice(first - c * TS + LANES, last - c * TS + LANES)
        prod = dot(u_high[:, first:last], tabs["cols"][inside, :])
        prod = prod[:, : 2 * band] + prod[:, 2 * band :]
        prod = prod + dot(u_low[:, first:last], tabs["cols"][inside, : 2 * band])
        for k in range(2):
            own, other = prod[:band, k * band : (k + 1) * band], prod[band:, k * band : (k + 1) * band]
            half = own - sign * pltpu.roll(other, freqs, 1)
            spectrum[c, k] = half
            spectrum[c, 2 + k] = pltpu.roll(half, freqs, 1) * sign

    def lane_block(value, k):
        return value[:, k * band : (k + 1) * band]

    pairs = group // 2
    state = {}

    def gather(c, first, i):
        for k in (2 * i, 2 * i + 1):
            down = shift[0, first + k] + reach
            along = shift[1, first + k] + reach
            rows = pl.ds(down, freqs)
            close = residue >= along
            upper = jnp.where(close, spectrum[c, 0, rows, :], spectrum[c, 1, rows, :])
            lower = jnp.where(close, spectrum[c, 2, rows, :], spectrum[c, 3, rows, :])
            scaled = pupils[first + k]
            high, low = split(jnp.concatenate([upper * scaled, lower * scaled], axis=0))
            lifts[c, :band, k * band : (k + 1) * band] = high
            lifts[c, band:, k * band : (k + 1) * band] = low

    def lift(c, first, i):
        lifted = dot(tabs["up_rows"][...], lifts[c, :, 2 * i * band : 2 * (i + 1) * band])
        high, low = split(lifted[:coarse] + lifted[coarse:])
        for k in range(2):
            lines[c, 2 * i + k, :, :band] = lane_block(high, k)
            lines[c, 2 * i + k, :, band:] = lane_block(low, k)

    def light_up(c, first, i):
        for k in (2 * i, 2 * i + 1):
            along = shift[1, first + k] + reach
            flip = jnp.where(residue >= along, 1.0, -1.0).astype(bf16)
            line = lines[c, k]
            even = dot(line, tabs["up_cols"][0])
            odd = dot(line * jnp.concatenate([flip, flip], axis=1), tabs["up_cols"][1])
            field = jnp.concatenate(
                [even[:, :coarse] + even[:, coarse:], odd[:, :coarse] + odd[:, coarse:]], axis=1
            )
            fields[c % plan.stores, first + k] = field
            state["power", c] = state["power", c] + field * field

    def fine_steps(c):
        def begin():
            power = state.pop(("power", c))
            even, odd = power[:, :coarse], power[:, coarse:]
            power = jnp.where(first_half, even + pltpu.roll(even, freqs, 1), odd + pltpu.roll(odd, freqs, 1))
            high, low = split(power)
            pair = jnp.concatenate([high, low], axis=1)
            state["quad", c] = jnp.concatenate([pair, pair], axis=0)

        def rows_of(m):
            return slice(m * FINE, (m + 1) * FINE)

        def weave_rows(m):
            left = dot(tabs["weave_rows"][rows_of(m), :], state["quad", c])
            high, low = split(left[:, :coarse] + left[:, coarse:])
            state["a", c, m] = jnp.concatenate([high, low], axis=1)

        def slope_rows(m):
            light = dot(state.pop(("a", c, m)), tabs["weave_up"][...])
            light = light[:, :TS] + light[:, TS:]
            bend = jnp.tanh((0.5 * resist_gain) * light - 0.5 * resist_gain * resist_level)
            wanted = target_v[rows_of(m), c * TS : (c + 1) * TS]
            slope = ((0.25 * resist_gain) * (bend + 1.0) - (0.5 * resist_gain) * wanted) * (1.0 - bend * bend)
            state["g", c, m] = split(slope)

        def fold_rows(m):
            high, low = state.pop(("g", c, m))
            part = dot(high, tabs["weave_cols"][...]) + dot(low, tabs["weave_cols"][...])
            high, low = split(part[:, :coarse] + part[:, coarse:])
            woven[c, rows_of(m), :] = jnp.concatenate([high, low], axis=1)

        def finish():
            part = dot(tabs["weave_down"][...], woven[c])
            part = part[:coarse] + part[coarse:]
            pull = 2.0 * (part[:, :coarse] + part[:, coarse:])
            turned = pltpu.roll(pull, freqs, 1)
            state["pull", c] = jnp.concatenate(
                [jnp.where(first_half, pull, turned), jnp.where(first_half, turned, pull)], axis=1
            )

        stages = (weave_rows, slope_rows, fold_rows)
        count = TS // FINE
        middle = [
            functools.partial(stages[k], t - k)
            for t in range(count + 2) for k in (2, 1, 0) if 0 <= t - k < count
        ]
        return [begin] + middle + [finish]

    def fall(c, first, i):
        for k in (2 * i, 2 * i + 1):
            high, low = split(fields[c % plan.stores, first + k] * state["pull", c])
            sums = []
            for h in range(2):
                left = jnp.concatenate([lane_block(high, h), lane_block(low, h)], axis=1)
                part = dot(left, tabs["down_cols"][h])
                sums.append(part[:, :band] + part[:, band:])
            along = shift[1, first + k] + reach
            flip = jnp.where(residue >= along, 1.0, -1.0).astype(f32)
            high, low = split(sums[0] + flip * sums[1])
            lifts[c, :band, k * band : (k + 1) * band] = high
            lifts[c, band:, k * band : (k + 1) * band] = low

    def settle(c, first, i):
        part = dot(tabs["down_rows"][...], lifts[c, :, 2 * i * band : 2 * (i + 1) * band])
        part = part[:band] + part[band:]
        for k in range(2):
            s = first + 2 * i + k
            mine = lane_block(part, k)
            mine = (mine[:freqs] + sign * pltpu.roll(mine[freqs:], freqs, 1)) * pupils[s]
            rows = pl.ds(shift[0, s] + reach, freqs)
            close = residue >= shift[1, s] + reach
            zero = jnp.zeros_like(mine)
            grads[c, 0, rows, :] += jnp.where(close, mine, zero)
            grads[c, 1, rows, :] += jnp.where(close, zero, mine)

    def steps(stage, c, first=0):
        return [functools.partial(stage, c, first, i) for i in range(pairs)]

    grads[...] = jnp.zeros_like(grads)
    tiles = range(plan.tile_cols)
    rounds = sources // group
    if rounds == 1:
        for c in tiles:
            state["power", c] = jnp.zeros((coarse, 2 * coarse), f32)
        stages = [
            lambda c: [functools.partial(transform, c)],
            lambda c: steps(gather, c),
            lambda c: steps(lift, c),
            lambda c: steps(light_up, c),
            fine_steps,
            lambda c: steps(fall, c),
            lambda c: steps(settle, c),
        ]
        wants = {
            2: ("up_rows", "up_cols"),
            4: ("target", "weave_rows", "weave_up", "weave_cols", "weave_down"),
            5: ("down_rows", "down_cols"),
        }
        for t in range(len(stages) + LAG * (plan.tile_cols - 1)):
            need(*wants.get(t, ()))
            run(merged(*[stages[t - LAG * c](c) for c in tiles if 0 <= t - LAG * c < len(stages)]))
    else:
        need(*(name for name in names if not name.startswith("final")))
        for c in tiles:
            transform(c)

            def forward(g, power):
                state["power", c] = power
                for stage in (gather, lift, light_up):
                    run(steps(stage, c, g * group))
                return state["power", c]

            def backward(g, carry):
                for stage in (fall, settle):
                    run(steps(stage, c, g * group))
                return carry

            state["power", c] = lax.fori_loop(0, rounds, forward, jnp.zeros((coarse, 2 * coarse), f32))
            run(fine_steps(c))
            lax.fori_loop(0, rounds, backward, 0)

    need("final_cols", "final_rows")
    wide = plan.wide
    bands = jnp.concatenate([grads[c, k] for c in range(plan.tile_cols) for k in range(2)], axis=1)
    high, low = split(bands)
    part = dot(high, final_tab[...])
    part = part[:, : 2 * wide] + part[:, 2 * wide :] + dot(low, final_tab[:, : 2 * wide])
    high, low = split(jnp.concatenate([part[:, :wide], part[:, wide:]], axis=0))
    rows_high, rows_low = tabs["final_rows"][0], tabs["final_rows"][1]
    final = dot(rows_high, high) + dot(rows_high, low) + dot(rows_low, high)
    whole_grad[...] = final[:, : plan.width]
    rim_start = pl.multiple_of(jnp.where(tile_row == 0, HALO + TS, 0), HALO)
    ends = [
        pltpu.make_async_copy(whole_grad.at[pl.ds(rim_start, HALO)], row_out, sems.at[0]),
        pltpu.make_async_copy(whole_grad.at[pl.ds(HALO, TS)], own_out, sems.at[1]),
    ]
    for end in ends:
        end.start()
    for end in ends:
        end.wait()


def local_image(plan, mask, target, pupil, source_shift, source_weight, halo):
    tables = plan.tables()
    chunks = {f"mask{i}": mask for i in range(plan.cols // CHUNK)}
    arrays = {"pupil": pupil, "e_own": tables["e_own"], "e_rim": tables["e_rim"], "halo": halo}
    arrays.update(chunks)
    arrays.update((n, tables[n]) for n in ("cols", "up_rows", "up_cols", "weave_rows", "weave_up"))
    arrays["target"] = target
    arrays.update((n, t) for n, t in tables.items() if n not in arrays)
    names = tuple(arrays)
    picked = ("e_rim", "final_cols")
    local = {n: a.shape[1:] if n in picked else a.shape for n, a in arrays.items()}
    local.update({n: (TS, CHUNK) for n in chunks})
    smem = pl.BlockSpec(memory_space=pltpu.SMEM)
    distant = pl.BlockSpec(memory_space=pltpu.MemorySpace.HBM)
    sources, group, tile_cols = plan.sources, plan.group, plan.tile_cols
    band, coarse = plan.band, plan.coarse
    return pl.pallas_call(
        functools.partial(image_kernel, plan, names),
        out_shape=[
            jax.ShapeDtypeStruct((TS, plan.width), f32),
            jax.ShapeDtypeStruct((HALO, plan.width), f32),
        ],
        in_specs=[smem, smem] + [distant] * len(names),
        out_specs=[distant] * 2,
        scratch_shapes=[pltpu.VMEM(local[n], arrays[n].dtype) for n in names]
        + [
            pltpu.VMEM((sources, plan.freqs, band), f32),
            pltpu.VMEM((tile_cols, 4, band, band), f32),
            pltpu.VMEM((plan.stores, sources, coarse, 2 * coarse), f32),
            pltpu.VMEM((tile_cols, 2, band, band), f32),
            pltpu.VMEM((PAD, plan.width), f32),
            pltpu.VMEM((2 * band, plan.cols), bf16),
            pltpu.VMEM((2 * band, plan.cols), bf16),
            pltpu.VMEM((tile_cols, TS, 2 * coarse), bf16),
            pltpu.VMEM((tile_cols, 2 * band, group * band), bf16),
            pltpu.VMEM((tile_cols, group, coarse, 2 * band), bf16),
            pltpu.SemaphoreType.DMA((len(names),)),
        ],
        compiler_params=pltpu.CompilerParams(vmem_limit_bytes=60 * 1024 * 1024),
        name="image",
    )(source_shift.T, source_weight, *[jnp.asarray(arrays[n]) for n in names])


def shards(plan, mask, target, pupil, source_shift, source_weight):
    tile_row = lax.axis_index("tile")
    swap = [(0, 1), (1, 0)]
    edge = lax.dynamic_slice_in_dim(mask, jnp.where(tile_row == 0, TS - HALO, 0), HALO, 0)
    halo = lax.ppermute(edge, "tile", swap)
    own, row = local_image(plan, mask, target, pupil, source_shift, source_weight, halo)
    row = lax.ppermute(row, "tile", swap)
    first = jnp.where(tile_row == 0, TS - HALO, 0)
    return lax.dynamic_update_slice_in_dim(own, lax.dynamic_slice_in_dim(own, first, HALO, 0) + row, first, 0)


def solution(mesh):
    sizes = dict(mesh.shape)

    def run(mask, target, pupil, source_shift, source_weight):
        plan = Plan(pupil.shape[0], mask.shape[1], sizes["src"], source_shift.shape[0])
        placed = (P(("groups", "tile"), None), P(("groups", "tile"), None), P(), P(), P())
        return jax.shard_map(
            functools.partial(shards, plan),
            mesh=mesh,
            in_specs=placed,
            out_specs=P(("groups", "tile"), "src"),
            check_vma=False,
        )(mask, target, pupil, source_shift, source_weight)

    return run
```

time: 25.1 us -> 22.2 us (0.88)
  Pallas kernels: 19.2 us -> 15.5 us
  other arithmetic: 0 us -> 1.38 us
  local copies, waits for them, and re-layouts: 2.26 us -> 1.66 us
    pallas_call x1, Pallas kernels: 17.8 us -> 15.5 us  [local_image(): pl.pallas_call(functools.partial(image_kernel, plan, names), out_shape=[j...]
    pallas_call x1 -> x0, Pallas kernels: 1.41 us -> none  [shards(): pl.pallas_call(finish_kernel, out_shape=jax.ShapeDtypeStruct((TS, plan.wi...]
    dynamic_update_slice x0 -> x1, other arithmetic: none -> 1.38 us  [shards(): lax.dynamic_update_slice_in_dim(own, lax.dynamic_slice_in_dim(own, first,...]
    unnamed x4 -> x2, local copies, waits for them, and re-layouts: 1.3 us -> 0.69 us
where the time goes in v2:
time: 22.2 us; the launch traced here: 22 us
  Pallas kernels  15.5 us (70%)
  waiting for transfers between devices  2.23 us (10%)
  local copies, waits for them, and re-layouts  1.66 us (7%)
  other arithmetic  1.38 us (6%)
  starting transfers between devices  1.18 us (5%)
    pallas_call x1, Pallas kernels, local_image(): pl.pallas_call(functools.partial(image_kernel, plan, names), out_shape=[j...  15.5 us
    dynamic_update_slice x1, other arithmetic, shards(): lax.dynamic_update_slice_in_dim(own, lax.dynamic_slice_in_dim(own, first,...  1.38 us
    ppermute x1, waiting for transfers between devices, shards(): halo = lax.ppermute(edge, 'tile', swap)  1.16 us
    ppermute x1, waiting for transfers between devices, shards(): row = lax.ppermute(row, 'tile', swap)  1.07 us
    dynamic_slice x1, local copies, waits for them, and re-layouts, shards(): lax.dynamic_slice_in_dim(mask, jnp.where(tile_row == 0, TS - HALO, 0), HA...  0.97 us
    ppermute x1, starting transfers between devices, shards(): halo = lax.ppermute(edge, 'tile', swap)  0.74 us
    unnamed x2, local copies, waits for them, and re-layouts  0.69 us
  transfers between devices with their start and end apart: 2, of which 2 were waited for; matrix products, arithmetic and copies ran while one was open for 0% of the time, Pallas kernels for 0%

profile of v2, /device:TPU:13, one launch (start us, length us, event | category | flops | bytes accessed | tf_op | source)
XLA Modules:
  0.0 22.0 jit_solution(10867253641631706674)
XLA Ops:
  0.0 1.0 %constant_dynamic-slice_fusion = f32[64,1024]{1,0:T(8,128)S(1)} fusion(f32[512,1024]{1,0:T(8,128)} %refs_4_.1, s32[]{:T(128)S(6)} %select_n.8), kind=kLoop, calls=%fused_computation.1 | loop fusion | bytes 524292 | tf_op jit(solution)/shard_map/dynamic_slice | solution.py:469
  1.0 0.7 %collective-permute-start = (f32[64,1024]{1,0:T(8,128)S(1)}, f32[64,1024]{1,0:T(8,128)S(1)}, u32[]{:S(2)}, u32[]{:S(2)}) collective-permute-start(f32[64,1024]{1,0:T(8,128)S(1)} %constant_dynamic-slice_fusion), channel_id=1, source_target_pairs={{0,1},{1,0},{2,3},{3,2},{4,5},{5,4},{6,7},{7,6},{8,9},{9,8},{10,11... | collective-permute-start | bytes 786440 | tf_op jit(solution)/shard_map/ppermute | solution.py:470
  1.7 1.2 %collective-permute-done.refs_3_ = f32[64,1024]{1,0:T(8,128)S(1)} collective-permute-done((f32[64,1024]{1,0:T(8,128)S(1)}, f32[64,1024]{1,0:T(8,128)S(1)}, u32[]{:S(2)}, u32[]{:S(2)}) %collective-permute-start) | collective-permute-done | bytes 262176 | tf_op jit(solution)/shard_map/ppermute | solution.py:470
  2.9 0.0 copy-start
  2.9 0.7 %copy-done = f32[64,1024]{1,0:T(8,128)} copy-done((f32[64,1024]{1,0:T(8,128)}, f32[64,1024]{1,0:T(8,128)S(1)}, u32[]{:S(2)}) %copy-start) | copy-done | bytes 262168
  3.6 15.5 %image.1 = (f32[512,128]{1,0:T(8,128)}, f32[64,128]{1,0:T(8,128)}) custom-call(s32[2,24]{1,0:T(2,128)} %bitcast.1, f32[24]{0:T(128)} %weight.1, f32[64,64]{1,0:T(8,128)} %refs_0_.1, bf16[512,512]{1,0:T(8,128)(2,1)} %constant.36.clone.refs_1_, bf16[2,256,192]{2,1,0:T(8,128)(2,1)} %constant.37.clone.refs_2_, f32[64,1024]{1,0:T(8,128)} %copy-done, ...), custom_call_target="tpu_custom_call" | custom-call | tf_op jit(solution)/shard_map/image/pallas_call | solution.py:439
  19.1 0.4 %collective-permute-start.1 = (f32[64,128]{1,0:T(8,128)}, f32[64,128]{1,0:T(8,128)S(1)}, u32[]{:S(2)}, u32[]{:S(2)}) collective-permute-start(f32[64,128]{1,0:T(8,128)} %get-tuple-element.8), channel_id=1, source_target_pairs={{0,1},{1,0},{2,3},{3,2},{4,5},{5,4},{6,7},{7,6},{8,9},{9,8},{10,11... | collective-permute-start | bytes 98312 | tf_op jit(solution)/shard_map/ppermute | solution.py:472
  19.5 1.1 %collective-permute-done.1 = f32[64,128]{1,0:T(8,128)S(1)} collective-permute-done((f32[64,128]{1,0:T(8,128)}, f32[64,128]{1,0:T(8,128)S(1)}, u32[]{:S(2)}, u32[]{:S(2)}) %collective-permute-start.1) | collective-permute-done | bytes 32800 | tf_op jit(solution)/shard_map/ppermute | solution.py:472
  20.6 1.4 %add_dynamic-update-slice_fusion = f32[512,128]{1,0:T(8,128)} fusion(f32[512,128]{1,0:T(8,128)} %get-tuple-element.7, s32[]{:T(128)S(6)} %select_n.8, f32[64,128]{1,0:T(8,128)S(1)} %collective-permute-done.1), kind=kLoop, calls=%fused_computation | loop fusion | flops 8192 | bytes 98308 | tf_op jit(solution)/shard_map/dynamic_update_slice | solution.py:474
Async XLA Ops:
  1.0 1.9 %collective-permute-start = (f32[64,1024]{1,0:T(8,128)S(1)}, f32[64,1024]{1,0:T(8,128)S(1)}, u32[]{:S(2)}, u32[]{:S(2)}) collective-permute-start(f32[64,1024]{1,0:T(8,128)S(1)} %constant_dynamic-slice_fusion), channel_id=1, source_target_pairs={{0,1},{1,0},{2,3},{3,2},{4,5},{5,4},{6,7},{7,6},{8,9},{9,8},{10,11... | collective-permute-start | bytes 786440 | tf_op jit(solution)/shard_map/ppermute | solution.py:470
  2.9 0.7 %copy-start = (f32[64,1024]{1,0:T(8,128)}, f32[64,1024]{1,0:T(8,128)S(1)}, u32[]{:S(2)}) copy-start(f32[64,1024]{1,0:T(8,128)S(1)} %collective-permute-done.refs_3_) | copy-start | bytes 786436
  19.1 1.5 %collective-permute-start.1 = (f32[64,128]{1,0:T(8,128)}, f32[64,128]{1,0:T(8,128)S(1)}, u32[]{:S(2)}, u32[]{:S(2)}) collective-permute-start(f32[64,128]{1,0:T(8,128)} %get-tuple-element.8), channel_id=1, source_target_pairs={{0,1},{1,0},{2,3},{3,2},{4,5},{5,4},{6,7},{7,6},{8,9},{9,8},{10,11... | collective-permute-start | bytes 98312 | tf_op jit(solution)/shard_map/ppermute | solution.py:472

commit v3 on v2

--- a/solution.py
+++ b/solution.py
@@ -15,7 +15,7 @@
 PAD = TS + 2 * HALO
 LANES = 128
 FINE = 256
-CHUNK = 1024
+CHUNK = 512
 LAG = 1
 MOST = 24
 
@@ -141,7 +141,8 @@
                 )
             blocks.append(both(np.concatenate(pieces, axis=0), 1))
         out["final_cols"] = np.stack(blocks)
-        out["final_rows"] = np.stack(halves(rows.T))
+        out["own_rows"] = np.stack(halves(rows.T[HALO : HALO + TS]))
+        out["final_rows"] = np.stack([both(rows.T[HALO + TS :], 0), both(rows.T[:HALO], 0)])
         return {name: np.ascontiguousarray(value) for name, value in out.items()}
 
 
@@ -157,25 +158,25 @@
 
 def image_kernel(plan, names, shift, weight, *refs):
     far = dict(zip(names, refs[: len(names)]))
-    own_out, row_out = refs[len(names) : len(names) + 2]
+    tail_out, row_out = refs[len(names) : len(names) + 2]
     near = dict(zip(names, refs[len(names) + 2 :]))
     (
-        pupils, spectrum, fields, grads, whole_grad, u_high, u_low, woven, lifts, lines, sems,
+        pupils, spectrum, fields, grads, tail, rim, u_high, u_low, woven, lifts, lines, sems,
     ) = refs[2 * len(names) + 2 :]
     sources, group = plan.sources, plan.group
     freqs, reach, band, coarse = plan.freqs, plan.reach, plan.band, plan.coarse
     tile_row = lax.axis_index("tile")
     block = lax.axis_index("src")
-    picked = {"e_rim": tile_row, "final_cols": block}
+    picked = {"e_rim": tile_row, "final_cols": block, "final_rows": tile_row}
     pending = {}
+    spans = {f"mask{n}": slice(n, n + CHUNK) for n in range(0, plan.cols, CHUNK)}
     for i, name in enumerate(names):
         source = far[name].at[picked[name]] if name in picked else far[name]
-        if name.startswith("mask"):
-            source = far[name].at[:, pl.ds(int(name[4:]) * CHUNK, CHUNK)]
+        if name in spans:
+            source = source.at[:, spans[name]]
         pending[name] = pltpu.make_async_copy(source, near[name], sems.at[i])
-    early = ("pupil", "e_own", "e_rim", "halo", "cols")
-    started = [name for name in names if name in early or name.startswith("mask")]
-    for name in started:
+    early = [name for name in names if name in ("pupil", "e_own", "e_rim", "halo", "cols") or name in spans]
+    for name in early:
         pending[name].start()
 
     def need(*wanted):
@@ -209,19 +210,17 @@
         lax.fori_loop(0, sources, lambda s, c: (place_pupil(s), c)[1], 0)
 
     need("e_own", "e_rim", "halo")
-    e_own, rim_table = tabs["e_own"], e_rim[...]
-    for i in range(0, plan.cols // CHUNK):
-        cols = slice(i * CHUNK, (i + 1) * CHUNK)
-        need(f"mask{i}")
-        if i == 0:
-            for name in names:
-                if name not in started:
-                    pending[name].start()
-        high, low = split(near[f"mask{i}"][...])
+    for name, cols in spans.items():
+        need(name)
+        if cols.start == 0:
+            for late in names:
+                if late not in early:
+                    pending[late].start()
         rim_high, rim_low = split(halo[:, cols])
-        rows = dot(rim_table, jnp.concatenate([rim_high, rim_high, rim_low], axis=0))
-        part = dot(e_own[...], high)
-        rows = rows + part[: 2 * band] + part[2 * band :] + dot(e_own[: 2 * band, :], low)
+        rows = dot(e_rim[...], jnp.concatenate([rim_high, rim_high, rim_low], axis=0))
+        high, low = split(near[name][...])
+        part = dot(near["e_own"][...], high)
+        rows = rows + part[: 2 * band] + part[2 * band :] + dot(near["e_own"][: 2 * band, :], low)
         high, low = split(rows)
         u_high[:, cols] = high
         u_low[:, cols] = low
@@ -405,33 +404,56 @@
     high, low = split(bands)
     part = dot(high, final_tab[...])
     part = part[:, : 2 * wide] + part[:, 2 * wide :] + dot(low, final_tab[:, : 2 * wide])
-    high, low = split(jnp.concatenate([part[:, :wide], part[:, wide:]], axis=0))
-    rows_high, rows_low = tabs["final_rows"][0], tabs["final_rows"][1]
-    final = dot(rows_high, high) + dot(rows_high, low) + dot(rows_low, high)
-    whole_grad[...] = final[:, : plan.width]
-    rim_start = pl.multiple_of(jnp.where(tile_row == 0, HALO + TS, 0), HALO)
-    ends = [
-        pltpu.make_async_copy(whole_grad.at[pl.ds(rim_start, HALO)], row_out, sems.at[0]),
-        pltpu.make_async_copy(whole_grad.at[pl.ds(HALO, TS)], own_out, sems.at[1]),
-    ]
-    for end in ends:
-        end.start()
+    column_part = jnp.concatenate([part[:, :wide], part[:, wide:]], axis=0)
+    tail[...] = column_part
+    ends = [pltpu.make_async_copy(tail, tail_out, sems.at[0]), pltpu.make_async_copy(rim, row_out, sems.at[1])]
+    ends[0].start()
+    high, low = split(column_part)
+    table = near["final_rows"]
+    part = dot(table[...], high)
+    part = part[:HALO] + part[HALO:] + dot(table[:HALO, :], low)
+    rim[...] = part[:, : plan.width]
+    ends[1].start()
     for end in ends:
         end.wait()
 
 
-def local_image(plan, mask, target, pupil, source_shift, source_weight, halo):
-    tables = plan.tables()
-    chunks = {f"mask{i}": mask for i in range(plan.cols // CHUNK)}
+def own_kernel(plan, tail, table, out):
+    high, low = split(tail[...])
+    part = dot(table[0], high) + dot(table[0], low) + dot(table[1], high)
+    out[...] = part[:, : plan.width]
+
+
+def add_kernel(own, row, out):
+    tile_row = lax.axis_index("tile")
+    out[...] = own[...]
+    first = pl.multiple_of(jnp.where(tile_row == 0, TS - HALO, 0), HALO)
+    out[pl.ds(first, HALO), :] = own[pl.ds(first, HALO), :] + row[...]
+
+
+def own_rows(plan, tables, tail):
+    vmem = pl.BlockSpec(memory_space=pltpu.VMEM)
+    return pl.pallas_call(
+        functools.partial(own_kernel, plan),
+        out_shape=jax.ShapeDtypeStruct((TS, plan.width), f32),
+        in_specs=[vmem] * 2,
+        out_specs=vmem,
+        compiler_params=pltpu.CompilerParams(vmem_limit_bytes=8 * 1024 * 1024),
+        cost_estimate=pl.CostEstimate(flops=10**9, bytes_accessed=10**6, transcendentals=0),
+        name="own_rows",
+    )(tail, jnp.asarray(tables["own_rows"]))
+
+
+def local_image(plan, tables, mask, target, pupil, source_shift, source_weight, halo):
     arrays = {"pupil": pupil, "e_own": tables["e_own"], "e_rim": tables["e_rim"], "halo": halo}
-    arrays.update(chunks)
+    arrays.update((f"mask{n}", mask) for n in range(0, plan.cols, CHUNK))
     arrays.update((n, tables[n]) for n in ("cols", "up_rows", "up_cols", "weave_rows", "weave_up"))
     arrays["target"] = target
-    arrays.update((n, t) for n, t in tables.items() if n not in arrays)
+    arrays.update((n, t) for n, t in tables.items() if n not in arrays and n != "own_rows")
     names = tuple(arrays)
-    picked = ("e_rim", "final_cols")
+    picked = ("e_rim", "final_cols", "final_rows")
     local = {n: a.shape[1:] if n in picked else a.shape for n, a in arrays.items()}
-    local.update({n: (TS, CHUNK) for n in chunks})
+    local.update((n, (TS, CHUNK)) for n in names if n.startswith("mask"))
     smem = pl.BlockSpec(memory_space=pltpu.SMEM)
     distant = pl.BlockSpec(memory_space=pltpu.MemorySpace.HBM)
     sources, group, tile_cols = plan.sources, plan.group, plan.tile_cols
@@ -439,7 +461,7 @@
     return pl.pallas_call(
         functools.partial(image_kernel, plan, names),
         out_shape=[
-            jax.ShapeDtypeStruct((TS, plan.width), f32),
+            jax.ShapeDtypeStruct((2 * band, plan.wide), f32),
             jax.ShapeDtypeStruct((HALO, plan.width), f32),
         ],
         in_specs=[smem, smem] + [distant] * len(names),
@@ -450,7 +472,8 @@
             pltpu.VMEM((tile_cols, 4, band, band), f32),
             pltpu.VMEM((plan.stores, sources, coarse, 2 * coarse), f32),
             pltpu.VMEM((tile_cols, 2, band, band), f32),
-            pltpu.VMEM((PAD, plan.width), f32),
+            pltpu.VMEM((2 * band, plan.wide), f32),
+            pltpu.VMEM((HALO, plan.width), f32),
             pltpu.VMEM((2 * band, plan.cols), bf16),
             pltpu.VMEM((2 * band, plan.cols), bf16),
             pltpu.VMEM((tile_cols, TS, 2 * coarse), bf16),
@@ -468,10 +491,19 @@
     swap = [(0, 1), (1, 0)]
     edge = lax.dynamic_slice_in_dim(mask, jnp.where(tile_row == 0, TS - HALO, 0), HALO, 0)
     halo = lax.ppermute(edge, "tile", swap)
-    own, row = local_image(plan, mask, target, pupil, source_shift, source_weight, halo)
+    tables = plan.tables()
+    tail, row = local_image(plan, tables, mask, target, pupil, source_shift, source_weight, halo)
     row = lax.ppermute(row, "tile", swap)
-    first = jnp.where(tile_row == 0, TS - HALO, 0)
-    return lax.dynamic_update_slice_in_dim(own, lax.dynamic_slice_in_dim(own, first, HALO, 0) + row, first, 0)
+    own = own_rows(plan, tables, tail)
+    vmem = pl.BlockSpec(memory_space=pltpu.VMEM)
+    return pl.pallas_call(
+        add_kernel,
+        out_shape=jax.ShapeDtypeStruct((TS, plan.width), f32),
+        in_specs=[vmem] * 2,
+        out_specs=vmem,
+        compiler_params=pltpu.CompilerParams(vmem_limit_bytes=8 * 1024 * 1024),
+        name="add_rows",
+    )(own, row)
 
 
 def solution(mesh):

time: 22.2 us -> 21.3 us (0.959)
  other arithmetic: 1.38 us -> 0 us
  waiting for transfers between devices: 2.23 us -> 1.16 us
  local copies, waits for them, and re-layouts: 1.66 us -> 2.58 us
  Pallas kernels: 15.5 us -> 16.2 us
    dynamic_update_slice x1 -> x0, other arithmetic: 1.38 us -> none  [shards(): lax.dynamic_update_slice_in_dim(own, lax.dynamic_slice_in_dim(own, first,...]
    pallas_call x0 -> x2, Pallas kernels: none -> 1.09 us  [the longest x1 0.73 us: shards(): pl.pallas_call(add_kernel, out_shape=jax.ShapeDtypeStruct((TS, plan.width...]
    ppermute x1, waiting for transfers between devices: 1.07 us -> 0.01 us  [shards(): row = lax.ppermute(row, 'tile', swap)]
    unnamed x2 -> x6, local copies, waits for them, and re-layouts: 0.69 us -> 1.61 us
    pallas_call x1, Pallas kernels: 15.5 us -> 15.1 us  [local_image(): pl.pallas_call(functools.partial(image_kernel, plan, names), out_shape=[j...]
  transfers between devices with their start and end apart: 2 -> 2, of which waited for: 2 -> 1; matrix products, arithmetic and copies ran while one was open for 0% -> 0% of each run, Pallas kernels for 0% -> 2%
where the time goes in v3:
time: 21.3 us; the launch traced here: 21.1 us
  Pallas kernels  16.2 us (76%)
  local copies, waits for them, and re-layouts  2.58 us (12%)
  starting transfers between devices  1.18 us (6%)
  waiting for transfers between devices  1.16 us (5%)
    pallas_call x1, Pallas kernels, local_image(): pl.pallas_call(functools.partial(image_kernel, plan, names), out_shape=[j...  15.1 us
    unnamed x6, local copies, waits for them, and re-layouts  1.61 us
    ppermute x1, waiting for transfers between devices, shards(): halo = lax.ppermute(edge, 'tile', swap)  1.16 us
    dynamic_slice x1, local copies, waits for them, and re-layouts, shards(): lax.dynamic_slice_in_dim(mask, jnp.where(tile_row == 0, TS - HALO, 0), HA...  0.97 us
    ppermute x1, starting transfers between devices, shards(): halo = lax.ppermute(edge, 'tile', swap)  0.74 us
    pallas_call x1, Pallas kernels, shards(): pl.pallas_call(add_kernel, out_shape=jax.ShapeDtypeStruct((TS, plan.width...  0.73 us
    ppermute x1, starting transfers between devices, shards(): row = lax.ppermute(row, 'tile', swap)  0.44 us
  transfers between devices with their start and end apart: 2, of which 1 were waited for; matrix products, arithmetic and copies ran while one was open for 0% of the time, Pallas kernels for 2%

profile of v3, /device:TPU:13, one launch (start us, length us, event | category | flops | bytes accessed | tf_op | source)
XLA Modules:
  0.0 21.1 jit_solution(16195446963322173467)
XLA Ops:
  0.0 1.0 %constant_dynamic-slice_fusion = f32[64,1024]{1,0:T(8,128)S(1)} fusion(f32[512,1024]{1,0:T(8,128)} %refs_5_.1, s32[]{:T(128)S(6)} %select_n.5), kind=kLoop, calls=%fused_computation | loop fusion | bytes 524292 | tf_op jit(solution)/shard_map/dynamic_slice | solution.py:492
  1.0 0.7 %collective-permute-start = (f32[64,1024]{1,0:T(8,128)S(1)}, f32[64,1024]{1,0:T(8,128)S(1)}, u32[]{:S(2)}, u32[]{:S(2)}) collective-permute-start(f32[64,1024]{1,0:T(8,128)S(1)} %constant_dynamic-slice_fusion), channel_id=1, source_target_pairs={{0,1},{1,0},{2,3},{3,2},{4,5},{5,4},{6,7},{7,6},{8,9},{9,8},{10,11... | collective-permute-start | bytes 786440 | tf_op jit(solution)/shard_map/ppermute | solution.py:493
  1.7 1.2 %collective-permute-done.refs_3_ = f32[64,1024]{1,0:T(8,128)S(1)} collective-permute-done((f32[64,1024]{1,0:T(8,128)S(1)}, f32[64,1024]{1,0:T(8,128)S(1)}, u32[]{:S(2)}, u32[]{:S(2)}) %collective-permute-start) | collective-permute-done | bytes 262176 | tf_op jit(solution)/shard_map/ppermute | solution.py:493
  2.9 0.0 copy-start.2
  2.9 0.7 %copy-done.2 = f32[64,1024]{1,0:T(8,128)} copy-done((f32[64,1024]{1,0:T(8,128)}, f32[64,1024]{1,0:T(8,128)S(1)}, u32[]{:S(2)}) %copy-start.2) | copy-done | bytes 262168
  3.6 0.0 copy-start.1
  3.6 15.1 %image.1 = (f32[256,128]{1,0:T(8,128)}, f32[64,128]{1,0:T(8,128)}) custom-call(s32[2,24]{1,0:T(2,128)} %bitcast.1, f32[24]{0:T(128)} %weight.1, f32[64,64]{1,0:T(8,128)} %refs_0_.1, bf16[512,512]{1,0:T(8,128)(2,1)} %constant.38.clone.refs_1_, bf16[2,256,192]{2,1,0:T(8,128)(2,1)} %constant.39.clone.refs_2_, f32[64,1024]{1,0:T(8,128)} %copy-done.2, ...), custom_call_target="tpu_custom_call" | custom-call | tf_op jit(solution)/shard_map/image/pallas_call | solution.py:461
  18.7 0.4 %collective-permute-start.1 = (f32[64,128]{1,0:T(8,128)}, f32[64,128]{1,0:T(8,128)S(1)}, u32[]{:S(2)}, u32[]{:S(2)}) collective-permute-start(f32[64,128]{1,0:T(8,128)} %get-tuple-element.8), channel_id=1, source_target_pairs={{0,1},{1,0},{2,3},{3,2},{4,5},{5,4},{6,7},{7,6},{8,9},{9,8},{10,11... | collective-permute-start | bytes 98312 | tf_op jit(solution)/shard_map/ppermute | solution.py:496
  19.1 0.0 copy-done.1
  19.1 0.0 copy-start
  19.1 0.9 %copy-done = f32[256,128]{1,0:T(8,128)S(1)} copy-done((f32[256,128]{1,0:T(8,128)S(1)}, f32[256,128]{1,0:T(8,128)}, u32[]{:S(2)}) %copy-start) | copy-done | bytes 131096
  20.0 0.4 %own_rows.1.own = f32[512,128]{1,0:T(8,128)S(1)} custom-call(f32[256,128]{1,0:T(8,128)S(1)} %copy-done, bf16[2,512,256]{2,1,0:T(8,128)(2,1)S(1)} %copy-done.1), custom_call_target="tpu_custom_call" | custom-call | flops 1000000000 | bytes 1000000 | tf_op jit(solution)/shard_map/own_rows/pallas_call | solution.py:436
  20.4 0.0 collective-permute-done.1.row
  20.4 0.7 %add_rows.1 = f32[512,128]{1,0:T(8,128)} custom-call(f32[512,128]{1,0:T(8,128)S(1)} %own_rows.1.own, f32[64,128]{1,0:T(8,128)S(1)} %collective-permute-done.1.row), custom_call_target="tpu_custom_call" | custom-call | tf_op jit(solution)/shard_map/add_rows/pallas_call | solution.py:499
Async XLA Ops:
  1.0 1.9 %collective-permute-start = (f32[64,1024]{1,0:T(8,128)S(1)}, f32[64,1024]{1,0:T(8,128)S(1)}, u32[]{:S(2)}, u32[]{:S(2)}) collective-permute-start(f32[64,1024]{1,0:T(8,128)S(1)} %constant_dynamic-slice_fusion), channel_id=1, source_target_pairs={{0,1},{1,0},{2,3},{3,2},{4,5},{5,4},{6,7},{7,6},{8,9},{9,8},{10,11... | collective-permute-start | bytes 786440 | tf_op jit(solution)/shard_map/ppermute | solution.py:493
  2.9 0.7 %copy-start.2 = (f32[64,1024]{1,0:T(8,128)}, f32[64,1024]{1,0:T(8,128)S(1)}, u32[]{:S(2)}) copy-start(f32[64,1024]{1,0:T(8,128)S(1)} %collective-permute-done.refs_3_) | copy-start | bytes 786436
  3.6 15.5 %copy-start.1 = (bf16[2,512,256]{2,1,0:T(8,128)(2,1)S(1)}, bf16[2,512,256]{2,1,0:T(8,128)(2,1)}, u32[]{:S(2)}) copy-start(bf16[2,512,256]{2,1,0:T(8,128)(2,1)} %constant.51.clone.table) | copy-start | bytes 1572868
  18.7 1.7 %collective-permute-start.1 = (f32[64,128]{1,0:T(8,128)}, f32[64,128]{1,0:T(8,128)S(1)}, u32[]{:S(2)}, u32[]{:S(2)}) collective-permute-start(f32[64,128]{1,0:T(8,128)} %get-tuple-element.8), channel_id=1, source_target_pairs={{0,1},{1,0},{2,3},{3,2},{4,5},{5,4},{6,7},{7,6},{8,9},{9,8},{10,11... | collective-permute-start | bytes 98312 | tf_op jit(solution)/shard_map/ppermute | solution.py:496
  19.1 0.9 %copy-start = (f32[256,128]{1,0:T(8,128)S(1)}, f32[256,128]{1,0:T(8,128)}, u32[]{:S(2)}) copy-start(f32[256,128]{1,0:T(8,128)} %get-tuple-element.7.tail) | copy-start | bytes 393220

commit v4 on v3

--- a/solution.py
+++ b/solution.py
@@ -156,18 +156,24 @@
         step()
 
 
-def image_kernel(plan, names, shift, weight, *refs):
+def image_kernel(plan, names, shift_far, weight_far, *refs):
     far = dict(zip(names, refs[: len(names)]))
     tail_out, row_out = refs[len(names) : len(names) + 2]
     near = dict(zip(names, refs[len(names) + 2 :]))
     (
-        pupils, spectrum, fields, grads, tail, rim, u_high, u_low, woven, lifts, lines, sems,
+        pupils, spectrum, fields, grads, tail, rim, u_high, u_low, woven, lifts, lines, shift, weight, sems,
     ) = refs[2 * len(names) + 2 :]
     sources, group = plan.sources, plan.group
     freqs, reach, band, coarse = plan.freqs, plan.reach, plan.band, plan.coarse
     tile_row = lax.axis_index("tile")
     block = lax.axis_index("src")
     picked = {"e_rim": tile_row, "final_cols": block, "final_rows": tile_row}
+    scalars = [
+        pltpu.make_async_copy(shift_far, shift, sems.at[len(names)]),
+        pltpu.make_async_copy(weight_far, weight, sems.at[len(names) + 1]),
+    ]
+    for copy in scalars:
+        copy.start()
     pending = {}
     spans = {f"mask{n}": slice(n, n + CHUNK) for n in range(0, plan.cols, CHUNK)}
     for i, name in enumerate(names):
@@ -188,6 +194,8 @@
     target_v, e_rim, final_tab, halo = (
         near[name] for name in ("target", "e_rim", "final_cols", "halo")
     )
+    for copy in scalars:
+        copy.wait()
     total = weight[0]
     for s in range(1, sources):
         total = total + weight[s]
@@ -454,7 +462,6 @@
     picked = ("e_rim", "final_cols", "final_rows")
     local = {n: a.shape[1:] if n in picked else a.shape for n, a in arrays.items()}
     local.update((n, (TS, CHUNK)) for n in names if n.startswith("mask"))
-    smem = pl.BlockSpec(memory_space=pltpu.SMEM)
     distant = pl.BlockSpec(memory_space=pltpu.MemorySpace.HBM)
     sources, group, tile_cols = plan.sources, plan.group, plan.tile_cols
     band, coarse = plan.band, plan.coarse
@@ -464,7 +471,7 @@
             jax.ShapeDtypeStruct((2 * band, plan.wide), f32),
             jax.ShapeDtypeStruct((HALO, plan.width), f32),
         ],
-        in_specs=[smem, smem] + [distant] * len(names),
+        in_specs=[distant] * (2 + len(names)),
         out_specs=[distant] * 2,
         scratch_shapes=[pltpu.VMEM(local[n], arrays[n].dtype) for n in names]
         + [
@@ -479,7 +486,9 @@
             pltpu.VMEM((tile_cols, TS, 2 * coarse), bf16),
             pltpu.VMEM((tile_cols, 2 * band, group * band), bf16),
             pltpu.VMEM((tile_cols, group, coarse, 2 * band), bf16),
-            pltpu.SemaphoreType.DMA((len(names),)),
+            pltpu.SMEM(source_shift.shape[::-1], jnp.int32),
+            pltpu.SMEM(source_weight.shape, f32),
+            pltpu.SemaphoreType.DMA((len(names) + 2,)),
         ],
         compiler_params=pltpu.CompilerParams(vmem_limit_bytes=60 * 1024 * 1024),
         name="image",

time: 21.3 us -> 20.6 us (0.967)
  Pallas kernels: 16.2 us -> 15.5 us
    pallas_call x1, Pallas kernels: 15.1 us -> 14.4 us  [local_image(): pl.pallas_call(functools.partial(image_kernel, plan, names), out_shape=[j...]
where the time goes in v4:
time: 20.6 us; the launch traced here: 20.4 us
  Pallas kernels  15.5 us (75%)
  local copies, waits for them, and re-layouts  2.58 us (13%)
  starting transfers between devices  1.17 us (6%)
  waiting for transfers between devices  1.16 us (6%)
    pallas_call x1, Pallas kernels, local_image(): pl.pallas_call(functools.partial(image_kernel, plan, names), out_shape=[j...  14.4 us
    unnamed x6, local copies, waits for them, and re-layouts  1.61 us
    ppermute x1, waiting for transfers between devices, shards(): halo = lax.ppermute(edge, 'tile', swap)  1.16 us
    dynamic_slice x1, local copies, waits for them, and re-layouts, shards(): lax.dynamic_slice_in_dim(mask, jnp.where(tile_row == 0, TS - HALO, 0), HA...  0.97 us
    ppermute x1, starting transfers between devices, shards(): halo = lax.ppermute(edge, 'tile', swap)  0.74 us
    pallas_call x1, Pallas kernels, shards(): pl.pallas_call(add_kernel, out_shape=jax.ShapeDtypeStruct((TS, plan.width...  0.73 us
    ppermute x1, starting transfers between devices, shards(): row = lax.ppermute(row, 'tile', swap)  0.43 us
  transfers between devices with their start and end apart: 2, of which 1 were waited for; matrix products, arithmetic and copies ran while one was open for 0% of the time, Pallas kernels for 2%

profile of v4, /device:TPU:13, one launch (start us, length us, event | category | flops | bytes accessed | tf_op | source)
XLA Modules:
  0.0 20.4 jit_solution(7603852655909125478)
XLA Ops:
  0.0 1.0 %constant_dynamic-slice_fusion = f32[64,1024]{1,0:T(8,128)S(1)} fusion(f32[512,1024]{1,0:T(8,128)} %refs_5_.1, s32[]{:T(128)S(6)} %select_n.5), kind=kLoop, calls=%fused_computation | loop fusion | bytes 524292 | tf_op jit(solution)/shard_map/dynamic_slice | solution.py:501
  1.0 0.7 %collective-permute-start = (f32[64,1024]{1,0:T(8,128)S(1)}, f32[64,1024]{1,0:T(8,128)S(1)}, u32[]{:S(2)}, u32[]{:S(2)}) collective-permute-start(f32[64,1024]{1,0:T(8,128)S(1)} %constant_dynamic-slice_fusion), channel_id=1, source_target_pairs={{0,1},{1,0},{2,3},{3,2},{4,5},{5,4},{6,7},{7,6},{8,9},{9,8},{10,11... | collective-permute-start | bytes 786440 | tf_op jit(solution)/shard_map/ppermute | solution.py:502
  1.7 1.2 %collective-permute-done.refs_3_ = f32[64,1024]{1,0:T(8,128)S(1)} collective-permute-done((f32[64,1024]{1,0:T(8,128)S(1)}, f32[64,1024]{1,0:T(8,128)S(1)}, u32[]{:S(2)}, u32[]{:S(2)}) %collective-permute-start) | collective-permute-done | bytes 262176 | tf_op jit(solution)/shard_map/ppermute | solution.py:502
  2.9 0.0 copy-start.2
  2.9 0.7 %copy-done.2 = f32[64,1024]{1,0:T(8,128)} copy-done((f32[64,1024]{1,0:T(8,128)}, f32[64,1024]{1,0:T(8,128)S(1)}, u32[]{:S(2)}) %copy-start.2) | copy-done | bytes 262168
  3.6 0.0 copy-start.1
  3.6 14.4 %image.1 = (f32[256,128]{1,0:T(8,128)}, f32[64,128]{1,0:T(8,128)}) custom-call(s32[2,24]{1,0:T(2,128)} %bitcast.1, f32[24]{0:T(128)} %weight_far.1, f32[64,64]{1,0:T(8,128)} %refs_0_.1, bf16[512,512]{1,0:T(8,128)(2,1)} %constant.38.clone.refs_1_, bf16[2,256,192]{2,1,0:T(8,128)(2,1)} %constant.39.clone.refs_2_, f32[64,1024]{1,0:T(8,128)} %copy-done.2, ...), custom_call_target="tpu_custom_call" | custom-call | tf_op jit(solution)/shard_map/image/pallas_call | solution.py:468
  18.0 0.4 %collective-permute-start.1 = (f32[64,128]{1,0:T(8,128)}, f32[64,128]{1,0:T(8,128)S(1)}, u32[]{:S(2)}, u32[]{:S(2)}) collective-permute-start(f32[64,128]{1,0:T(8,128)} %get-tuple-element.8), channel_id=1, source_target_pairs={{0,1},{1,0},{2,3},{3,2},{4,5},{5,4},{6,7},{7,6},{8,9},{9,8},{10,11... | collective-permute-start | bytes 98312 | tf_op jit(solution)/shard_map/ppermute | solution.py:505
  18.4 0.0 copy-done.1
  18.4 0.0 copy-start
  18.4 0.9 %copy-done = f32[256,128]{1,0:T(8,128)S(1)} copy-done((f32[256,128]{1,0:T(8,128)S(1)}, f32[256,128]{1,0:T(8,128)}, u32[]{:S(2)}) %copy-start) | copy-done | bytes 131096
  19.3 0.4 %own_rows.1.own = f32[512,128]{1,0:T(8,128)S(1)} custom-call(f32[256,128]{1,0:T(8,128)S(1)} %copy-done, bf16[2,512,256]{2,1,0:T(8,128)(2,1)S(1)} %copy-done.1), custom_call_target="tpu_custom_call" | custom-call | flops 1000000000 | bytes 1000000 | tf_op jit(solution)/shard_map/own_rows/pallas_call | solution.py:444
  19.7 0.0 collective-permute-done.1.row
  19.7 0.7 %add_rows.1 = f32[512,128]{1,0:T(8,128)} custom-call(f32[512,128]{1,0:T(8,128)S(1)} %own_rows.1.own, f32[64,128]{1,0:T(8,128)S(1)} %collective-permute-done.1.row), custom_call_target="tpu_custom_call" | custom-call | tf_op jit(solution)/shard_map/add_rows/pallas_call | solution.py:508
Async XLA Ops:
  1.0 1.9 %collective-permute-start = (f32[64,1024]{1,0:T(8,128)S(1)}, f32[64,1024]{1,0:T(8,128)S(1)}, u32[]{:S(2)}, u32[]{:S(2)}) collective-permute-start(f32[64,1024]{1,0:T(8,128)S(1)} %constant_dynamic-slice_fusion), channel_id=1, source_target_pairs={{0,1},{1,0},{2,3},{3,2},{4,5},{5,4},{6,7},{7,6},{8,9},{9,8},{10,11... | collective-permute-start | bytes 786440 | tf_op jit(solution)/shard_map/ppermute | solution.py:502
  2.9 0.7 %copy-start.2 = (f32[64,1024]{1,0:T(8,128)}, f32[64,1024]{1,0:T(8,128)S(1)}, u32[]{:S(2)}) copy-start(f32[64,1024]{1,0:T(8,128)S(1)} %collective-permute-done.refs_3_) | copy-start | bytes 786436
  3.6 14.8 %copy-start.1 = (bf16[2,512,256]{2,1,0:T(8,128)(2,1)S(1)}, bf16[2,512,256]{2,1,0:T(8,128)(2,1)}, u32[]{:S(2)}) copy-start(bf16[2,512,256]{2,1,0:T(8,128)(2,1)} %constant.51.clone.table) | copy-start | bytes 1572868
  18.0 1.7 %collective-permute-start.1 = (f32[64,128]{1,0:T(8,128)}, f32[64,128]{1,0:T(8,128)S(1)}, u32[]{:S(2)}, u32[]{:S(2)}) collective-permute-start(f32[64,128]{1,0:T(8,128)} %get-tuple-element.8), channel_id=1, source_target_pairs={{0,1},{1,0},{2,3},{3,2},{4,5},{5,4},{6,7},{7,6},{8,9},{9,8},{10,11... | collective-permute-start | bytes 98312 | tf_op jit(solution)/shard_map/ppermute | solution.py:505
  18.4 0.9 %copy-start = (f32[256,128]{1,0:T(8,128)S(1)}, f32[256,128]{1,0:T(8,128)}, u32[]{:S(2)}) copy-start(f32[256,128]{1,0:T(8,128)} %get-tuple-element.7.tail) | copy-start | bytes 393220

commit v5 on v4

--- a/solution.py
+++ b/solution.py
@@ -383,9 +383,15 @@
             4: ("target", "weave_rows", "weave_up", "weave_cols", "weave_down"),
             5: ("down_rows", "down_cols"),
         }
+        slots = []
         for t in range(len(stages) + LAG * (plan.tile_cols - 1)):
+            slots.append([stages[t - LAG * c](c) for c in tiles if 0 <= t - LAG * c < len(stages)])
+        falls, settles, half = slots[-2].pop(), slots.pop()[0], (pairs + 1) // 2
+        slots[-1].append(falls[:half])
+        slots += [[falls[half:], settles[:half]], [settles[half:]]]
+        for t, slot in enumerate(slots):
             need(*wants.get(t, ()))
-            run(merged(*[stages[t - LAG * c](c) for c in tiles if 0 <= t - LAG * c < len(stages)]))
+            run(merged(*slot))
     else:
         need(*(name for name in names if not name.startswith("final")))
         for c in tiles:

time: 20.6 us -> 20.5 us (level)
  no operation moved by 1% of the time
where the time goes in v5:
time: 20.5 us; the launch traced here: 20.4 us
  Pallas kernels  15.4 us (75%)
  local copies, waits for them, and re-layouts  2.58 us (13%)
  starting transfers between devices  1.18 us (6%)
  waiting for transfers between devices  1.16 us (6%)
    pallas_call x1, Pallas kernels, local_image(): pl.pallas_call(functools.partial(image_kernel, plan, names), out_shape=[j...  14.3 us
    unnamed x6, local copies, waits for them, and re-layouts  1.61 us
    ppermute x1, waiting for transfers between devices, shards(): halo = lax.ppermute(edge, 'tile', swap)  1.16 us
    dynamic_slice x1, local copies, waits for them, and re-layouts, shards(): lax.dynamic_slice_in_dim(mask, jnp.where(tile_row == 0, TS - HALO, 0), HA...  0.97 us
    ppermute x1, starting transfers between devices, shards(): halo = lax.ppermute(edge, 'tile', swap)  0.74 us
    pallas_call x1, Pallas kernels, shards(): pl.pallas_call(add_kernel, out_shape=jax.ShapeDtypeStruct((TS, plan.width...  0.73 us
    ppermute x1, starting transfers between devices, shards(): row = lax.ppermute(row, 'tile', swap)  0.44 us
  transfers between devices with their start and end apart: 2, of which 1 were waited for; matrix products, arithmetic and copies ran while one was open for 0% of the time, Pallas kernels for 2%

profile of v5, /device:TPU:13, one launch (start us, length us, event | category | flops | bytes accessed | tf_op | source)
XLA Modules:
  0.0 20.4 jit_solution(6530252956197868970)
XLA Ops:
  0.0 1.0 %constant_dynamic-slice_fusion = f32[64,1024]{1,0:T(8,128)S(1)} fusion(f32[512,1024]{1,0:T(8,128)} %refs_5_.1, s32[]{:T(128)S(6)} %select_n.5), kind=kLoop, calls=%fused_computation | loop fusion | bytes 524292 | tf_op jit(solution)/shard_map/dynamic_slice | solution.py:507
  1.0 0.7 %collective-permute-start = (f32[64,1024]{1,0:T(8,128)S(1)}, f32[64,1024]{1,0:T(8,128)S(1)}, u32[]{:S(2)}, u32[]{:S(2)}) collective-permute-start(f32[64,1024]{1,0:T(8,128)S(1)} %constant_dynamic-slice_fusion), channel_id=1, source_target_pairs={{0,1},{1,0},{2,3},{3,2},{4,5},{5,4},{6,7},{7,6},{8,9},{9,8},{10,11... | collective-permute-start | bytes 786440 | tf_op jit(solution)/shard_map/ppermute | solution.py:508
  1.7 1.2 %collective-permute-done.refs_3_ = f32[64,1024]{1,0:T(8,128)S(1)} collective-permute-done((f32[64,1024]{1,0:T(8,128)S(1)}, f32[64,1024]{1,0:T(8,128)S(1)}, u32[]{:S(2)}, u32[]{:S(2)}) %collective-permute-start) | collective-permute-done | bytes 262176 | tf_op jit(solution)/shard_map/ppermute | solution.py:508
  2.9 0.0 copy-start.2
  2.9 0.7 %copy-done.2 = f32[64,1024]{1,0:T(8,128)} copy-done((f32[64,1024]{1,0:T(8,128)}, f32[64,1024]{1,0:T(8,128)S(1)}, u32[]{:S(2)}) %copy-start.2) | copy-done | bytes 262168
  3.6 0.0 copy-start.1
  3.6 14.3 %image.1 = (f32[256,128]{1,0:T(8,128)}, f32[64,128]{1,0:T(8,128)}) custom-call(s32[2,24]{1,0:T(2,128)} %bitcast.1, f32[24]{0:T(128)} %weight_far.1, f32[64,64]{1,0:T(8,128)} %refs_0_.1, bf16[512,512]{1,0:T(8,128)(2,1)} %constant.38.clone.refs_1_, bf16[2,256,192]{2,1,0:T(8,128)(2,1)} %constant.39.clone.refs_2_, f32[64,1024]{1,0:T(8,128)} %copy-done.2, ...), custom_call_target="tpu_custom_call" | custom-call | tf_op jit(solution)/shard_map/image/pallas_call | solution.py:474
  17.9 0.4 %collective-permute-start.1 = (f32[64,128]{1,0:T(8,128)}, f32[64,128]{1,0:T(8,128)S(1)}, u32[]{:S(2)}, u32[]{:S(2)}) collective-permute-start(f32[64,128]{1,0:T(8,128)} %get-tuple-element.8), channel_id=1, source_target_pairs={{0,1},{1,0},{2,3},{3,2},{4,5},{5,4},{6,7},{7,6},{8,9},{9,8},{10,11... | collective-permute-start | bytes 98312 | tf_op jit(solution)/shard_map/ppermute | solution.py:511
  18.4 0.0 copy-done.1
  18.4 0.0 copy-start
  18.4 0.9 %copy-done = f32[256,128]{1,0:T(8,128)S(1)} copy-done((f32[256,128]{1,0:T(8,128)S(1)}, f32[256,128]{1,0:T(8,128)}, u32[]{:S(2)}) %copy-start) | copy-done | bytes 131096
  19.3 0.4 %own_rows.1.own = f32[512,128]{1,0:T(8,128)S(1)} custom-call(f32[256,128]{1,0:T(8,128)S(1)} %copy-done, bf16[2,512,256]{2,1,0:T(8,128)(2,1)S(1)} %copy-done.1), custom_call_target="tpu_custom_call" | custom-call | flops 1000000000 | bytes 1000000 | tf_op jit(solution)/shard_map/own_rows/pallas_call | solution.py:450
  19.6 0.0 collective-permute-done.1.row
  19.6 0.7 %add_rows.1 = f32[512,128]{1,0:T(8,128)} custom-call(f32[512,128]{1,0:T(8,128)S(1)} %own_rows.1.own, f32[64,128]{1,0:T(8,128)S(1)} %collective-permute-done.1.row), custom_call_target="tpu_custom_call" | custom-call | tf_op jit(solution)/shard_map/add_rows/pallas_call | solution.py:514
Async XLA Ops:
  1.0 1.9 %collective-permute-start = (f32[64,1024]{1,0:T(8,128)S(1)}, f32[64,1024]{1,0:T(8,128)S(1)}, u32[]{:S(2)}, u32[]{:S(2)}) collective-permute-start(f32[64,1024]{1,0:T(8,128)S(1)} %constant_dynamic-slice_fusion), channel_id=1, source_target_pairs={{0,1},{1,0},{2,3},{3,2},{4,5},{5,4},{6,7},{7,6},{8,9},{9,8},{10,11... | collective-permute-start | bytes 786440 | tf_op jit(solution)/shard_map/ppermute | solution.py:508
  2.9 0.7 %copy-start.2 = (f32[64,1024]{1,0:T(8,128)}, f32[64,1024]{1,0:T(8,128)S(1)}, u32[]{:S(2)}) copy-start(f32[64,1024]{1,0:T(8,128)S(1)} %collective-permute-done.refs_3_) | copy-start | bytes 786436
  3.6 14.8 %copy-start.1 = (bf16[2,512,256]{2,1,0:T(8,128)(2,1)S(1)}, bf16[2,512,256]{2,1,0:T(8,128)(2,1)}, u32[]{:S(2)}) copy-start(bf16[2,512,256]{2,1,0:T(8,128)(2,1)} %constant.51.clone.table) | copy-start | bytes 1572868
  17.9 1.7 %collective-permute-start.1 = (f32[64,128]{1,0:T(8,128)}, f32[64,128]{1,0:T(8,128)S(1)}, u32[]{:S(2)}, u32[]{:S(2)}) collective-permute-start(f32[64,128]{1,0:T(8,128)} %get-tuple-element.8), channel_id=1, source_target_pairs={{0,1},{1,0},{2,3},{3,2},{4,5},{5,4},{6,7},{7,6},{8,9},{9,8},{10,11... | collective-permute-start | bytes 98312 | tf_op jit(solution)/shard_map/ppermute | solution.py:511
  18.4 0.9 %copy-start = (f32[256,128]{1,0:T(8,128)S(1)}, f32[256,128]{1,0:T(8,128)}, u32[]{:S(2)}) copy-start(f32[256,128]{1,0:T(8,128)} %get-tuple-element.7.tail) | copy-start | bytes 393220
